TPU v7x, 256 devices: a whole 4x4x8 slice. The times are simulated.
256 devices in a mesh: inst: 32 (over y, z_hi, core), tp: 8 (over x, z_lo).
Axes of the slice: x: 4, y: 4, z: 8 (z_hi: 4, z_lo: 2; z = z_hi * 2 + z_lo), core: 2. Of those that a mesh axis runs over, the one named last changes fastest.
Arguments:
- queries: bfloat16 [8192, 8192], P('inst', 'tp'), may hold values from -160 to 160
- key_values: bfloat16 [8192, 2048], P('inst', 'tp'), may hold values from -8 to 8
- out_weight: bfloat16 [8192, 4096], P('tp'), may hold values from -0.0625 to 0.0625
- prompt_of: int32 [32], replicated, may hold values from 0 to 7, as said below
- cycle_rank: int32 [32], replicated, may hold values from 0 to 6, as said below
- span_len: int32 [32], replicated, may hold values from 129 to 256, as said below
- cache_slot: int32 [64], replicated, may hold values from 0 to 63, as said below
Outputs:
- mixed: bfloat16 [8192, 4096], P('inst', 'tp')
- decode_cache: bfloat16 [64, 128, 2048], P('inst', None, 'tp')
Inputs may be any that keep to these rules, and one draw needn't show every extreme that they name: `prompt_of`: every prompt number below 8 is served by one to seven instances. `cycle_rank`: the instances of one prompt hold the ranks 0, 1, 2 and so on, each once; some prompt has seven instances. `span_len`: some instance is full in every draw. `cache_slot`: A permutation of all cache slots. Slot s belongs to instance s // 2.
All inputs are finite; a program needn't handle non-finite values.
Results may differ from a plain program's by a relative error of at most 0.017.
Values may be sent and summed in bfloat16 or wider, within the bound.
A program may use at most 192 MiB of HBM per device.

v0:
```python
import math

import jax
import jax.numpy as jnp
from jax import lax
from jax.sharding import PartitionSpec as P

HD = 128
CACHE_BLOCKS = 2


NEG_LARGE = -1e30


def earlier_offsets(prompt_of, cycle_rank, span_len):
    same_cycle = prompt_of[None, :] == prompt_of[:, None]
    before = cycle_rank[None, :] < cycle_rank[:, None]
    return jnp.sum(jnp.where(same_cycle & before, span_len[None, :], 0), axis=1)


def lookup(table, index):
    match = index[:, None] == jnp.arange(table.shape[0], dtype=jnp.int32)[None, :]
    return jnp.sum(jnp.where(match, table[None, :], 0), axis=1)


def rounded(values):
    narrow = lax.optimization_barrier(values.astype(jnp.bfloat16))
    return narrow.astype(jnp.float32)


def on_device(queries, key_values, out_weight, prompt_of, cycle_rank, span_len, cache_slot):
    span = queries.shape[0]
    width = key_values.shape[1]
    local_kv = width // (2 * HD)
    local_heads = queries.shape[1] // HD
    group = local_heads // local_kv
    scale = 1.0 / math.sqrt(HD)
    myself = lax.axis_index("inst")
    devices = lax.axis_size("inst")
    blocks = CACHE_BLOCKS
    offsets = earlier_offsets(prompt_of, cycle_rank, span_len)
    my_prompt = prompt_of[myself]
    rows_here = jnp.arange(span, dtype=jnp.int32)
    query_live = rows_here < span_len[myself]
    query_pos = offsets[myself] + rows_here
    grouped = queries.reshape(span, local_kv, group, HD)
    order = jnp.arange(blocks, dtype=jnp.int32)
    piece = lax.all_gather(key_values, "inst", axis=0, tiled=True)
    best = jnp.full((local_kv, group, span), NEG_LARGE, jnp.float32)
    count = piece.shape[0]
    global_rows = jnp.arange(count, dtype=jnp.int32)
    source = global_rows // span
    inside = global_rows % span
    key_live = inside < lookup(span_len, source)
    key_pos = lookup(offsets, source) + inside
    same = lookup(prompt_of, source) == my_prompt
    allowed = (
        query_live[:, None] & (key_live & same)[None, :] & (key_pos[None, :] <= query_pos[:, None])
    )
    split = piece.reshape(count, local_kv, 2, HD)
    scores = (
        jnp.einsum("qkgd,rkd->kgqr", grouped, split[:, :, 0], preferred_element_type=jnp.float32)
        * scale
    )
    scores = jnp.where(allowed, scores, NEG_LARGE)
    fresh = jnp.maximum(best, jnp.max(scores, axis=-1))
    expos = jnp.where(allowed, jnp.exp(scores - fresh[..., None]), 0.0)
    total = jnp.sum(expos, axis=-1)
    numer = jnp.einsum(
        "kgqr,rkd->kgqd",
        expos.astype(jnp.bfloat16),
        split[:, :, 1],
        preferred_element_type=jnp.float32,
    )
    best, total, numer = (fresh, total, numer)
    mine = lax.dynamic_slice_in_dim(cache_slot, myself * blocks, blocks)
    target = mine // blocks
    within = mine % blocks
    position = jnp.sum(
        (target[None, :] == target[:, None]) & (order[None, :] < order[:, None]), axis=1
    )
    select = (jnp.arange(devices, dtype=jnp.int32)[:, None, None] == target[None, None, :]) & (
        order[None, :, None] == position[None, None, :]
    )
    select = select.reshape(devices * blocks, blocks)
    flat_rows = key_values.reshape(blocks, -1)
    outgoing = jnp.dot(
        select.astype(jnp.bfloat16), flat_rows, preferred_element_type=jnp.float32
    ).astype(jnp.bfloat16)
    outgoing = outgoing.reshape(devices, blocks, span // blocks, width)
    labels = jnp.where(
        jnp.any(select, axis=1), jnp.sum(jnp.where(select, within[None, :], 0), axis=1), -1
    )
    labels = labels.reshape(devices, blocks)
    arrived, arrived_labels = (
        lax.all_to_all(outgoing, "inst", split_axis=0, concat_axis=0, tiled=True),
        lax.all_to_all(labels, "inst", split_axis=0, concat_axis=0, tiled=True),
    )
    placing = (arrived_labels.reshape(1, -1) == order[:, None]).astype(jnp.bfloat16)
    decode_cache = jnp.dot(
        placing, arrived.reshape(devices * blocks, -1), preferred_element_type=jnp.float32
    ).astype(jnp.bfloat16)
    decode_cache = decode_cache.reshape(blocks, span // blocks, width)
    attended = numer / jnp.where(total > 0.0, total, 1.0)[..., None]
    attended = attended.transpose(2, 0, 1, 3).reshape(span, local_heads * HD).astype(jnp.bfloat16)
    partial_sum = rounded(jnp.dot(attended, out_weight, preferred_element_type=jnp.float32))
    mixed = lax.psum_scatter(
        partial_sum.astype(jnp.bfloat16), "tp", scatter_dimension=1, tiled=True
    )
    return (mixed, decode_cache)


def solution(mesh):
    placed = (P("inst", "tp"), P("inst", "tp"), P("tp", None), P(), P(), P(), P())
    return jax.shard_map(
        on_device,
        mesh=mesh,
        in_specs=placed,
        out_specs=(P("inst", "tp"), P("inst", None, "tp")),
        check_vma=False,
    )
```

profile of v0, /device:TPU:1, one launch (start us, length us, event | category | flops | bytes accessed | tf_op | source)
XLA Modules:
  0.0 273.2 jit_solution(2663877365011053481)
XLA Ops:
  7.2 0.0 copy-start
  7.2 0.0 copy-start.1
  7.2 0.0 copy-start.2
  7.2 0.0 all-gather.2.cloned.1.call-start
  7.2 1.7 copy.24
  9.0 0.0 all-gather.2.cloned.1.call-update
  9.0 0.7 and_select_fusion
  9.7 0.7 and_select_fusion.1
  10.5 0.2 fusion.21
  10.6 0.1 iota_compare_fusion.2
  10.7 0.1 iota_compare_fusion.1
  10.8 0.1 select_reduce_fusion.3
  10.9 0.1 and_reduce_fusion
  11.0 0.6 broadcast_select_fusion
  11.6 12.8 %all-to-all-start = ((s32[32,1,2]{2,1,0:T(1,128)}), s32[32,1,2]{2,1,0:T(1,128)S(1)}, u32[]{:S(2)}, u32[]{:S(2)}) async-start(s32[32,1,2]{2,1,0:T(1,128)} %bitcast.20), calls=%async_computation.1 | async-start | bytes 32768 | tf_op jit(solution)/shard_map/all_to_all | solution.py:97
  24.3 0.9 reshape.209
  25.3 1.3 dynamic_slice.13
  26.6 1.3 dynamic_slice.12
  27.9 0.9 select_reduce_fusion.4
  28.8 0.6 dynamic_slice.14
  29.4 0.1 and.115
  29.5 1.3 convolution_convert_fusion
  30.8 3.0 %copy.35 = bf16[8,8,128,256]{3,2,1,0:T(8,128)(2,1)} copy(bf16[8,8,128,256]{3,1,2,0:T(8,128)(2,1)S(1)} %bitcast.76) | data formatting | bytes 8388608
  33.8 0.6 iota_compare_fusion.3
  34.5 0.6 iota_add_fusion
  35.0 0.0 copy-done.1
  35.1 0.0 copy-done.2
  35.1 0.5 select_reduce_fusion.1
  35.6 0.7 fusion.19
  36.3 5.8 %compare_and_fusion = pred[256,8192]{0,1:T(8,128)(4,1)S(1)} fusion(s32[256]{0:T(256)S(1)} %iota_add_fusion, s32[8192]{0:T(1024)S(1)} %fusion.15, pred[256]{0:T(512)(128)(4,1)S(1)} %iota_compare_fusion.3, pred[8192]{0:T(1024)(128)(4,1)S(1)} %fusion.19), kind=kLoop, calls=%fused_computation.10 | loop fusion | flops 6291456 | bytes 2139392 | tf_op jit(solution)/shard_map/and | solution.py:58
  42.2 37.9 %all-gather.2.cloned.1.call-done = bf16[8192,256]{0,1:T(8,128)(2,1)} async-done(((bf16[256,256]{0,1:T(8,128)(2,1)}), bf16[8192,256]{0,1:T(8,128)(2,1)}) %all-gather.2.cloned.1.call-update) | async-done | bytes 4194320 | tf_op jit(solution)/shard_map/all_gather | solution.py:48
  80.0 0.0 copy-done
  80.0 25.0 %fusion = (f32[8,256]{1,0:T(8,128)S(1)}, f32[8192,256,8]{1,0,2:T(8,128)}) fusion(pred[256,8192]{0,1:T(8,128)(4,1)S(1)} %compare_and_fusion, bf16[8192,1,2,128]{0,3,2,1:T(8,128)(2,1)} %bitcast.81, bf16[256,1024]{1,0:T(8,128)(2,1)S(1)} %copy-done), kind=kOutput, calls=%fused_computation.2 | convolution fusion | flops 4345296896 | bytes 71835648 | tf_op jit(solution)/shard_map/qkgd,rkd->kgqr/dot_general | solution.py:62
  105.1 21.7 %fusion.1 = f32[8,256]{1,0:T(8,128)S(1)} fusion(f32[8192,256,8]{1,0,2:T(8,128)} %get-tuple-element.10, f32[8,256]{1,0:T(8,128)S(1)} %broadcast_maximum_fusion, pred[256,8192]{0,1:T(8,128)(4,1)S(1)} %compare_and_fusion), kind=kLoop, calls=%fused_computation.3 | loop fusion | flops 83884032 | bytes 69222400 | tf_op jit(solution)/shard_map/reduce_sum | solution.py:68
  126.8 0.0 all-to-all-done
  126.8 5.7 %all-to-all-start.1 = ((bf16[32,2,128,256]{3,2,1,0:T(8,128)(2,1)}), bf16[32,2,128,256]{3,2,1,0:T(8,128)(2,1)}, u32[]{:S(2)}, u32[]{:S(2)}) async-start(bf16[32,2,128,256]{3,2,1,0:T(8,128)(2,1)} %bitcast.75), calls=%async_computation.2 | async-start | bytes 8388608 | tf_op jit(solution)/shard_map/all_to_all | solution.py:96
  132.5 0.2 reduce-scatter.2.cloned.1.call-start
  132.8 24.7 %divide_convert_fusion = bf16[8,256,128]{1,2,0:T(8,128)(2,1)S(1)} fusion(f32[8192,256,8]{1,0,2:T(8,128)} %get-tuple-element.10, f32[8,256]{1,0:T(8,128)S(1)} %broadcast_maximum_fusion, pred[256,8192]{0,1:T(8,128)(4,1)S(1)} %compare_and_fusion, bf16[8192,1,2,128]{0,3,2,1:T(8,128)(2,1)} %bitcast.82, f32[8,256]{1,0:T(8,128)S(1)} %compare_select_fusion), kind=kOutput, calls=%fused_computation.15 | convolution fusion | flops 4379377664 | bytes 71843840 | tf_op jit(solution)/shard_map/kgqr,rkd->kgqd/dot_general | solution.py:69
  157.5 7.1 %convolution_convert_fusion.2 = bf16[256,4096]{1,0:T(8,128)(2,1)} fusion(bf16[256,1024]{0,1:T(8,128)(2,1)S(1)} %bitcast.78, bf16[1024,4096]{1,0:T(8,128)(2,1)} %param.9), kind=kOutput, calls=%fused_computation.11 | convolution fusion | flops 2148532224 | bytes 11010048 | tf_op jit(solution)/shard_map/dot_general | solution.py:106
  164.6 0.0 reduce-scatter.2.cloned.1.call-update
  164.7 0.5 broadcast.189
  165.2 0.7 reduce.7
  165.9 0.1 eq.147
  166.0 83.1 %all-to-all-done.1 = bf16[32,2,128,256]{3,2,1,0:T(8,128)(2,1)} async-done(((bf16[32,2,128,256]{3,2,1,0:T(8,128)(2,1)}), bf16[32,2,128,256]{3,2,1,0:T(8,128)(2,1)}, u32[]{:S(2)}, u32[]{:S(2)}) %all-to-all-start.1) | async-done | bytes 4194336 | tf_op jit(solution)/shard_map/all_to_all | solution.py:96
  249.1 4.8 %copy.36 = bf16[8,8,128,256]{3,1,2,0:T(8,128)(2,1)S(1)} copy(bf16[8,8,128,256]{3,2,1,0:T(8,128)(2,1)} %bitcast.30) | data formatting | bytes 8388608
  253.8 0.7 convolution_convert_fusion.1
  254.5 0.7 copy.45
  255.2 11.2 %reduce-scatter.2.cloned.1.call-done = bf16[256,512]{1,0:T(8,128)(2,1)} async-done(((bf16[256,4096]{1,0:T(8,128)(2,1)}), bf16[256,512]{1,0:T(8,128)(2,1)}) %reduce-scatter.2.cloned.1.call-update) | async-done | bytes 262160 | tf_op jit(solution)/shard_map/reduce_scatter | solution.py:107
  (4 shorter events, 0.0 us)
Async XLA Ops:
  7.2 72.9 %copy-start = (bf16[256,1024]{1,0:T(8,128)(2,1)S(1)}, bf16[256,1024]{1,0:T(8,128)(2,1)}, u32[]{:S(2)}) copy-start(bf16[256,1024]{1,0:T(8,128)(2,1)} %param.7) | copy-start | bytes 1572868
  7.2 27.9 %copy-start.1 = (s32[32]{0:T(128)S(1)}, s32[32]{0:T(128)}, u32[]{:S(2)}) copy-start(s32[32]{0:T(128)} %param.10) | copy-start | bytes 388
  7.2 27.9 %copy-start.2 = (s32[32]{0:T(128)S(1)}, s32[32]{0:T(128)}, u32[]{:S(2)}) copy-start(s32[32]{0:T(128)} %param.12) | copy-start | bytes 388
  7.2 72.8 %all-gather.2.cloned.1.call-start = ((), (), s32[]{:S(2)}) async-start(), calls=%async_computation.3 | async-start | bytes 4325376 | tf_op jit(solution)/shard_map/all_gather | solution.py:48
  11.6 115.2 %all-to-all-start = ((s32[32,1,2]{2,1,0:T(1,128)}), s32[32,1,2]{2,1,0:T(1,128)S(1)}, u32[]{:S(2)}, u32[]{:S(2)}) async-start(s32[32,1,2]{2,1,0:T(1,128)} %bitcast.20), calls=%async_computation.1 | async-start | bytes 32768 | tf_op jit(solution)/shard_map/all_to_all | solution.py:97
  126.8 122.3 %all-to-all-start.1 = ((bf16[32,2,128,256]{3,2,1,0:T(8,128)(2,1)}), bf16[32,2,128,256]{3,2,1,0:T(8,128)(2,1)}, u32[]{:S(2)}, u32[]{:S(2)}) async-start(bf16[32,2,128,256]{3,2,1,0:T(8,128)(2,1)} %bitcast.75), calls=%async_computation.2 | async-start | bytes 8388608 | tf_op jit(solution)/shard_map/all_to_all | solution.py:96
  132.5 133.8 %reduce-scatter.2.cloned.1.call-start = ((), (), s32[]{:S(2)}) async-start(), calls=%async_computation.4 | async-start | bytes 2359296 | tf_op jit(solution)/shard_map/reduce_scatter | solution.py:107
Sparse Core Ops, SparseCore 0:
  11.1 68.9 all-gather.1
  164.8 101.5 reduce-scatter.1
where the time goes:
time: 274 us; the launch traced here: 273 us
  waiting for transfers between devices  132 us (48%)
  matrix products  58.9 us (21%)
  other arithmetic  34.1 us (12%)
  starting transfers between devices  18.7 us (7%)
  local copies, waits for them, and re-layouts  15 us (5%)
  between operations  14.2 us (5%)
    all_to_all x1, waiting for transfers between devices, on_device(): lax.all_to_all(outgoing, 'inst', split_axis=0, concat_axis=0, tiled=True)  83.1 us
    all_gather x1, waiting for transfers between devices, on_device(): piece = lax.all_gather(key_values, 'inst', axis=0, tiled=True)  37.9 us
    dot_general x1, matrix products, on_device(): jnp.einsum('qkgd,rkd->kgqr', grouped, split[:, :, 0], preferred_element_t...  25 us
    dot_general x1, matrix products, on_device(): jnp.einsum('kgqr,rkd->kgqd', expos.astype(jnp.bfloat16), split[:, :, 1],...  24.7 us
    reduce_sum x1, other arithmetic, on_device(): total = jnp.sum(expos, axis=-1)  21.7 us
    all_to_all x1, starting transfers between devices, on_device(): lax.all_to_all(labels, 'inst', split_axis=0, concat_axis=0, tiled=True)  12.8 us
    reduce_scatter x1, waiting for transfers between devices, on_device(): lax.psum_scatter(partial_sum.astype(jnp.bfloat16), 'tp', scatter_dimensio...  11.2 us
    unnamed x10, local copies, waits for them, and re-layouts  10.2 us
  transfers between devices with their start and end apart: 4, of which 3 were waited for; matrix products, arithmetic and copies ran while one was open for 39% of the time, Pallas kernels for 0%

commit v1 on v0

v1 whole, which is shorter than its diff:
```python
import functools
import math

import jax
import jax.numpy as jnp
from jax import lax
from jax.experimental import pallas as pl
from jax.experimental.pallas import tpu as pltpu
from jax.sharding import PartitionSpec as P

HD = 128
SPAN = 256
HEADS = 8
EARLIER = 6
KEYS = (EARLIER + 1) * SPAN
CHUNK = 512
ZROWS = 160
XROWS = SPAN - ZROWS
NEG = -1e30
MESH = pl.DeviceIdType.MESH
COPIES = 96


def kernel(
    q_hbm, kv_hbm, w_hbm, prompt_hbm, rank_hbm, len_hbm, slot_hbm,
    mixed_hbm, cache_hbm,
    qbuf, kbuf, vbuf, wbuf, kcat, vcat, bias, probs, totals, att,
    zsend, zrecv, own1, xsend, xrecv, x2send, x2recv, own2, z2send, z2recv,
    mixbuf, cachebuf,
    prompt, rank, length, slot,
    local_sem, send_sem, recv_sem,
):
    me = lax.axis_index("inst")
    tp = lax.axis_index("tp")
    y, zh, core = me // 8, (me // 2) % 4, me % 2
    x, zl = tp // 2, tp % 2

    def inst_at(dy, dz, dc):
        return (((y + dy) % 4) * 4 + (zh + dz) % 4) * 2 + (core + dc) % 2

    def tp_at(dx, dz):
        return ((x + dx) % 4) * 2 + (zl + dz) % 2

    z_up, z_down = (inst_at(0, 1, 0), tp), (inst_at(0, 3, 0), tp)
    y_up, y_down = (inst_at(1, 0, 0), tp), (inst_at(3, 0, 0), tp)
    sibling = (inst_at(0, 0, 1), tp)
    z_pair = (me, tp_at(0, 1))
    x_peer = {dx: (me, tp_at(dx, 0)) for dx in (1, 2, 3)}

    n_local = [0]

    def local(src, dst):
        copy = pltpu.make_async_copy(src, dst, local_sem.at[n_local[0]])
        n_local[0] += 1
        copy.start()
        return copy

    own_k = local(kv_hbm.at[:, pl.ds(0, HD)], kbuf.at[0])
    own_v = local(kv_hbm.at[:, pl.ds(HD, HD)], vbuf.at[0])
    tables = [
        local(src, dst)
        for src, dst in (
            (prompt_hbm, prompt), (rank_hbm, rank), (len_hbm, length), (slot_hbm, slot)
        )
    ]
    q_copy = local(q_hbm, qbuf)

    barrier = pltpu.get_barrier_semaphore()
    friends = [z_up, z_down, y_up, y_down, sibling, z_pair] + list(x_peer.values())
    for friend in friends:
        pl.semaphore_signal(barrier, inc=1, device_id=friend, device_id_type=MESH)
    w_copies = {}
    for dz in (1, 0):
        for dx in (2, 1, 3, 0):
            columns = pl.ds(pl.multiple_of(tp_at(dx, dz) * CHUNK, CHUNK), CHUNK)
            w_copies[dx, dz] = local(w_hbm.at[:, columns], wbuf.at[dx * 2 + dz])
    pl.semaphore_wait(barrier, len(friends))

    sent = []

    def send(src, dst, device):
        index = len(sent)
        copy = pltpu.make_async_remote_copy(
            src_ref=src, dst_ref=dst, send_sem=send_sem.at[index], recv_sem=recv_sem.at[index],
            device_id=device, device_id_type=MESH,
        )
        copy.start()
        sent.append(copy)
        return copy

    own_k.wait()
    own_v.wait()
    z_k = {3: send(kbuf.at[0], kbuf.at[3], z_up), 1: send(kbuf.at[0], kbuf.at[1], z_down)}
    yu, yd = {}, {}

    def along_y(name, buf, dz):
        yu[name, dz] = send(buf.at[dz], buf.at[12 + dz], y_up)
        yd[name, dz] = send(buf.at[dz], buf.at[4 + dz], y_down)

    far = {}

    def onward(name, buf, dz):
        if dz < 2:
            yu[name, dz].wait_recv()
            far[name, dz] = send(buf.at[12 + dz], buf.at[8 + dz], y_up)
        else:
            yd[name, dz].wait_recv()
            far[name, dz] = send(buf.at[4 + dz], buf.at[8 + dz], y_down)

    def rest_near(name, dz):
        (yd if dz < 2 else yu)[name, dz].wait_recv()

    across = {}

    def to_sibling(name, buf, start, count):
        across[name, start] = send(
            buf.at[pl.ds(start, count)], buf.at[pl.ds(16 + start, count)], sibling
        )

    along_y("k", kbuf, 0)
    z_v = {3: send(vbuf.at[0], vbuf.at[3], z_up), 1: send(vbuf.at[0], vbuf.at[1], z_down)}
    along_y("v", vbuf, 0)
    to_sibling("k", kbuf, 0, 1)
    to_sibling("v", vbuf, 0, 1)

    z_k[3].wait_recv()
    z_k[2] = send(kbuf.at[3], kbuf.at[2], z_up)
    along_y("k", kbuf, 3)
    z_k[1].wait_recv()
    along_y("k", kbuf, 1)

    for copy in tables:
        copy.wait()
    my_prompt, my_rank, my_len = prompt[me], rank[me], length[me]

    who, live = [me] * EARLIER, [jnp.int32(0)] * EARLIER
    for j in range(32):
        same, its_rank, its_len = prompt[j] == my_prompt, rank[j], length[j]
        for s in range(EARLIER):
            hit = same & (its_rank == s) & (s < my_rank)
            who[s] = jnp.where(hit, j, who[s])
            live[s] = jnp.where(hit, its_len, live[s])
    block_of = [jnp.int32(0)] * 2
    for b in range(64):
        for s in range(2):
            block_of[s] = jnp.where(slot[b] == 2 * me + s, b, block_of[s])

    def place(j):
        dy = ((j >> 3) + 4 - y) & 3
        dz = (((j >> 1) & 3) + 4 - zh) & 3
        dc = ((j & 1) + 2 - core) & 1
        return dc * 16 + dy * 4 + dz

    lane = lax.broadcasted_iota(jnp.int32, (1, SPAN), 1)
    for s in range(EARLIER):
        bias[:, s * SPAN:(s + 1) * SPAN] = jnp.where(lane < live[s], 0.0, NEG)

    z_k[2].wait_recv()
    along_y("k", kbuf, 2)
    to_sibling("k", kbuf, 1, 3)
    z_v[3].wait_recv()
    z_v[1].wait_recv()
    z_v[2] = send(vbuf.at[1], vbuf.at[2], z_down)
    onward("k", kbuf, 0)
    along_y("v", vbuf, 3)
    along_y("v", vbuf, 1)
    onward("k", kbuf, 3)
    onward("k", kbuf, 1)
    onward("k", kbuf, 2)
    z_v[2].wait_recv()
    along_y("v", vbuf, 2)
    to_sibling("v", vbuf, 1, 3)
    for dz in range(4):
        rest_near("k", dz)
    to_sibling("k", kbuf, 4, 4)
    to_sibling("k", kbuf, 12, 4)
    onward("v", vbuf, 0)
    for dz in range(4):
        far["k", dz].wait_recv()
    to_sibling("k", kbuf, 8, 4)
    for start in (0, 1, 4, 12, 8):
        across["k", start].wait_recv()

    q_copy.wait()
    for s in range(EARLIER):
        kcat[s * SPAN:(s + 1) * SPAN, :] = kbuf[place(who[s])]
    kcat[EARLIER * SPAN:, :] = kbuf[0]
    rows = 128
    factor = math.log2(math.e) / math.sqrt(HD)

    def weigh(head):
        @pl.loop(0, SPAN // rows)
        def _(part):
            start = pl.multiple_of(part * rows, rows)
            scores = lax.dot_general(
                qbuf[pl.ds(start, rows), head * HD:(head + 1) * HD], kcat[...],
                (((1,), (1,)), ((), ())), preferred_element_type=jnp.float32,
            )
            earlier = scores[:, :EARLIER * SPAN] + bias[...]
            row = lax.broadcasted_iota(jnp.int32, (rows, SPAN), 0) + start
            column = lax.broadcasted_iota(jnp.int32, (rows, SPAN), 1)
            here = jnp.where(column <= row, scores[:, EARLIER * SPAN:], NEG)
            top = jnp.maximum(
                jnp.max(earlier, axis=1, keepdims=True), jnp.max(here, axis=1, keepdims=True)
            )
            earlier = jnp.exp2((earlier - top) * factor)
            here = jnp.exp2((here - top) * factor)
            total = jnp.sum(earlier, axis=1, keepdims=True) + jnp.sum(here, axis=1, keepdims=True)
            its_row = lax.broadcasted_iota(jnp.int32, (rows, 1), 0) + start
            inverse = jnp.where(its_row < my_len, 1.0 / total, 0.0)
            probs[head, pl.ds(start, rows), :EARLIER * SPAN] = earlier.astype(jnp.bfloat16)
            probs[head, pl.ds(start, rows), EARLIER * SPAN:] = here.astype(jnp.bfloat16)
            totals[head, pl.ds(start, rows), :] = jnp.broadcast_to(inverse, (rows, HD))

    def near_done():
        for dz in range(4):
            rest_near("v", dz)
        to_sibling("v", vbuf, 4, 4)
        to_sibling("v", vbuf, 12, 4)

    def far_done():
        for dz in range(4):
            far["v", dz].wait_recv()
        to_sibling("v", vbuf, 8, 4)

    between = {
        1: lambda: onward("v", vbuf, 3),
        2: lambda: onward("v", vbuf, 1),
        4: lambda: onward("v", vbuf, 2),
        5: near_done,
        7: far_done,
    }
    for head in range(HEADS):
        weigh(head)
        if head in between:
            between[head]()
    for start in (0, 1, 4, 12, 8):
        across["v", start].wait_recv()

    for s in range(EARLIER):
        vcat[s * SPAN:(s + 1) * SPAN, :] = vbuf[place(who[s])]
    vcat[EARLIER * SPAN:, :] = vbuf[0]
    for head in range(HEADS):
        numer = jnp.dot(probs[head], vcat[...], preferred_element_type=jnp.float32)
        att[:, head * HD:(head + 1) * HD] = (numer * totals[head]).astype(jnp.bfloat16)

    z1, x2 = {}, {}
    for dx in (2, 1, 3, 0):
        w_copies[dx, 1].wait()
        term = jnp.dot(att[...], wbuf[dx * 2 + 1], preferred_element_type=jnp.float32)
        zsend[dx] = term[:ZROWS].astype(jnp.bfloat16)
        z1[dx] = send(zsend.at[dx], zrecv.at[dx], z_pair)
        if dx:
            x2send[dx - 1, 1] = term[ZROWS:].astype(jnp.bfloat16)
            x2[dx, 1] = send(x2send.at[dx - 1, 1], x2recv.at[dx - 1, 1], x_peer[dx])
        else:
            own2[1] = term[ZROWS:]
    for dx in (2, 1, 3, 0):
        w_copies[dx, 0].wait()
        term = jnp.dot(att[...], wbuf[dx * 2], preferred_element_type=jnp.float32)
        own1[dx] = term[:ZROWS]
        if dx:
            x2send[dx - 1, 0] = term[ZROWS:].astype(jnp.bfloat16)
            x2[dx, 0] = send(x2send.at[dx - 1, 0], x2recv.at[dx - 1, 0], x_peer[dx])
        else:
            own2[0] = term[ZROWS:]

    x1 = {}

    def pass_on(dx):
        z1[dx].wait_recv()
        xsend[dx - 1] = (own1[dx] + zrecv[dx].astype(jnp.float32)).astype(jnp.bfloat16)
        x1[dx] = send(xsend.at[dx - 1], xrecv.at[dx - 1], x_peer[dx])

    pass_on(2)
    for dx in (1, 3, 2):
        x2[dx, 1].wait_recv()
    total = own2[1]
    for k in range(3):
        total = total + x2recv[k, 1].astype(jnp.float32)
    z2send[...] = total.astype(jnp.bfloat16)
    z2 = send(z2send, z2recv, z_pair)
    pass_on(1)

    for s in range(2):
        its, second = place(block_of[s] >> 1), (block_of[s] & 1) == 1
        for buf, at in ((kbuf, 0), (vbuf, HD)):
            block = buf[its]
            cachebuf[s, :, at:at + HD] = jnp.where(second, block[SPAN // 2:], block[:SPAN // 2])
    cache_copy = local(cachebuf, cache_hbm)
    pass_on(3)

    for dx in (1, 3, 2):
        x2[dx, 0].wait_recv()
    z2.wait_recv()
    total = own2[0] + z2recv[...].astype(jnp.float32)
    for k in range(3):
        total = total + x2recv[k, 0].astype(jnp.float32)
    mixbuf[ZROWS:, :] = total.astype(jnp.bfloat16)
    out_low = local(mixbuf.at[pl.ds(ZROWS, XROWS)], mixed_hbm.at[pl.ds(ZROWS, XROWS)])

    z1[0].wait_recv()
    for dx in (2, 1, 3):
        x1[dx].wait_recv()
    total = own1[0] + zrecv[0].astype(jnp.float32)
    for k in range(3):
        total = total + xrecv[k].astype(jnp.float32)
    mixbuf[:ZROWS, :] = total.astype(jnp.bfloat16)
    out_high = local(mixbuf.at[pl.ds(0, ZROWS)], mixed_hbm.at[pl.ds(0, ZROWS)])

    for copy in sent:
        copy.wait_send()
    cache_copy.wait()
    out_low.wait()
    out_high.wait()


def on_device(queries, key_values, out_weight, prompt_of, cycle_rank, span_len, cache_slot):
    bf16, f32 = jnp.bfloat16, jnp.float32
    width = HEADS * HD
    vmem = pltpu.VMEM
    return pl.pallas_call(
        kernel,
        out_shape=(
            jax.ShapeDtypeStruct((SPAN, CHUNK), bf16),
            jax.ShapeDtypeStruct((2, SPAN // 2, 2 * HD), bf16),
        ),
        in_specs=[pl.BlockSpec(memory_space=pl.ANY)] * 7,
        out_specs=[pl.BlockSpec(memory_space=pl.ANY)] * 2,
        scratch_shapes=[
            vmem((SPAN, width), bf16),
            vmem((32, SPAN, HD), bf16),
            vmem((32, SPAN, HD), bf16),
            vmem((8, width, CHUNK), bf16),
            vmem((KEYS, HD), bf16),
            vmem((KEYS, HD), bf16),
            vmem((1, EARLIER * SPAN), f32),
            vmem((HEADS, SPAN, KEYS), bf16),
            vmem((HEADS, SPAN, HD), f32),
            vmem((SPAN, width), bf16),
            vmem((4, ZROWS, CHUNK), bf16),
            vmem((4, ZROWS, CHUNK), bf16),
            vmem((4, ZROWS, CHUNK), f32),
            vmem((3, ZROWS, CHUNK), bf16),
            vmem((3, ZROWS, CHUNK), bf16),
            vmem((3, 2, XROWS, CHUNK), bf16),
            vmem((3, 2, XROWS, CHUNK), bf16),
            vmem((2, XROWS, CHUNK), f32),
            vmem((XROWS, CHUNK), bf16),
            vmem((XROWS, CHUNK), bf16),
            vmem((SPAN, CHUNK), bf16),
            vmem((2, SPAN // 2, 2 * HD), bf16),
            pltpu.SMEM((32,), jnp.int32),
            pltpu.SMEM((32,), jnp.int32),
            pltpu.SMEM((32,), jnp.int32),
            pltpu.SMEM((64,), jnp.int32),
            pltpu.SemaphoreType.DMA((24,)),
            pltpu.SemaphoreType.DMA((COPIES,)),
            pltpu.SemaphoreType.DMA((COPIES,)),
        ],
        compiler_params=pltpu.CompilerParams(
            collective_id=0, has_side_effects=True, vmem_limit_bytes=56 * 1024 * 1024
        ),
        cost_estimate=pl.CostEstimate(
            flops=4 * SPAN * HEADS * KEYS * HD + 2 * SPAN * width * 4096,
            bytes_accessed=10 * 1024 * 1024,
            transcendentals=HEADS * SPAN * KEYS,
        ),
    )(queries, key_values, out_weight, prompt_of, cycle_rank, span_len, cache_slot)


def solution(mesh):
    placed = (P("inst", "tp"), P("inst", "tp"), P("tp", None), P(), P(), P(), P())
    return jax.shard_map(
        on_device,
        mesh=mesh,
        in_specs=placed,
        out_specs=(P("inst", "tp"), P("inst", None, "tp")),
        check_vma=False,
    )
```

time: 274 us -> 67.7 us (0.25)
  waiting for transfers between devices: 132 us -> 0 us
  Pallas kernels: 0 us -> 63.1 us
  matrix products: 58.9 us -> 0 us
  other arithmetic: 34.1 us -> 0 us
  starting transfers between devices: 18.7 us -> 0 us
  between operations: 14.2 us -> 0.64 us
  local copies, waits for them, and re-layouts: 15 us -> 3.24 us
    all_to_all x2 -> x0, waiting for transfers between devices: 83.1 us -> none  [the longest x1 83.1 us: on_device(): lax.all_to_all(outgoing, 'inst', split_axis=0, concat_axis=0, tiled=True)]
    pallas_call x0 -> x1, Pallas kernels: none -> 63.1 us  [on_device(): pl.pallas_call(kernel, out_shape=(jax.ShapeDtypeStruct((SPAN, CHUNK), bf1...]
    dot_general x5 -> x0, matrix products: 58.9 us -> none  [the longest x1 25 us: on_device(): jnp.einsum('qkgd,rkd->kgqr', grouped, split[:, :, 0], preferred_element_t...]
    all_gather x1 -> x0, waiting for transfers between devices: 37.9 us -> none  [on_device(): piece = lax.all_gather(key_values, 'inst', axis=0, tiled=True)]
    reduce_sum x5 -> x0, other arithmetic: 23.4 us -> none  [the longest x1 21.7 us: on_device(): total = jnp.sum(expos, axis=-1)]
    all_to_all x2 -> x0, starting transfers between devices: 18.5 us -> none  [the longest x1 12.8 us: on_device(): lax.all_to_all(labels, 'inst', split_axis=0, concat_axis=0, tiled=True)]
    reduce_scatter x1 -> x0, waiting for transfers between devices: 11.2 us -> none  [on_device(): lax.psum_scatter(partial_sum.astype(jnp.bfloat16), 'tp', scatter_dimensio...]
    unnamed x10 -> x2, local copies, waits for them, and re-layouts: 10.2 us -> 3.24 us
  transfers between devices with their start and end apart: 4 -> 0, of which waited for: 3 -> 0; matrix products, arithmetic and copies ran while one was open for 39% -> 0% of each run, Pallas kernels for 0% -> 0%
where the time goes in v1:
time: 67.7 us; the launch traced here: 67 us
  Pallas kernels  63.1 us (93%)
  local copies, waits for them, and re-layouts  3.24 us (5%)
    pallas_call x1, Pallas kernels, on_device(): pl.pallas_call(kernel, out_shape=(jax.ShapeDtypeStruct((SPAN, CHUNK), bf1...  63.1 us
    unnamed x2, local copies, waits for them, and re-layouts  3.24 us

profile of v1, /device:TPU:1, one launch (start us, length us, event | category | flops | bytes accessed | tf_op | source)
XLA Modules:
  0.0 67.0 jit_solution(14051304133346300673)
XLA Ops:
  0.6 63.1 %shard_map.86 = (bf16[256,512]{1,0:T(8,128)(2,1)}, bf16[2,128,256]{2,1,0:T(8,128)(2,1)}) custom-call(bf16[256,1024]{1,0:T(8,128)(2,1)} %q_hbm.1, bf16[256,256]{1,0:T(8,128)(2,1)} %kv_hbm.1, bf16[1024,4096]{1,0:T(8,128)(2,1)} %w_hbm.1, s32[32]{0:T(128)} %prompt_hbm.1, s32[32]{0:T(128)} %rank_hbm.1, s32[32]{0:T(128)} %len_hbm.1, s32[64]{0:T(128)} %slot_hbm.1), custom_call_target="tpu_custom_call" | custom-call | flops 4026531840 | bytes 10485760 | tf_op jit(solution)/shard_map/pallas_call | solution.py:322
  63.8 1.7 %copy.11 = bf16[256,512]{1,0:T(8,128)(2,1)} copy(bf16[256,512]{1,0:T(8,128)(2,1)} %get-tuple-element.4) | data formatting | bytes 524288
  65.5 1.6 %copy.12 = bf16[2,128,256]{2,1,0:T(8,128)(2,1)} copy(bf16[2,128,256]{2,1,0:T(8,128)(2,1)} %get-tuple-element.5) | data formatting | bytes 262144

commit v2 on v1

--- a/solution.py
+++ b/solution.py
@@ -20,13 +20,23 @@
 MESH = pl.DeviceIdType.MESH
 COPIES = 96
 
+PLAN = (
+    "+zk3", "+zk1", "+k0u", "+k0d", "+v0d", "?k0u", "+v0u", "+zv1", "?zk3", "+k3d", "?zk1", "+k1u",
+    "+zk2", "?v0d", "+fk0", "?k0d", "?v0u", "+k1d", "?zv1", "+v1d", "+k3u", "+zv2", "+xv0", "?k1u",
+    "+zv3", "?zk2", "+k2d", "+fk1", "+xk0", "+xk1", "?xk1", "?k3d", "+fk3", "?k1d", "+k2u", "?k3u",
+    "?v1d", "?k2d", "+fk2", "?zv2", "+v2u", "+xk4", "?xk0", "?xv0", "?zv3", "+xv1", "+v3u", "?xk4",
+    "?k2u", "+v3d", "?fk3", "+fv1", "?fk0", "?fk1", "+xk12", "?xv1", "+xk8", "?fk2", "+xk10",
+    "+v1u", "?xk8", "+v2d", "+fv0", "?v2u", "?xk12", "+fv2", "?xk10", "#", "?v3u", "#", "+fv3",
+    "#", "#", "?v1u", "+xv12", "#", "?fv2", "#", "?fv1", "?v3d", "?fv0", "+xv8", "?fv3", "?v2d",
+    "+xv4", "?xv12", "+xv10", "#", "#", "?xv10", "?xv8", "?xv4",
+)
+
 
 def kernel(
     q_hbm, kv_hbm, w_hbm, prompt_hbm, rank_hbm, len_hbm, slot_hbm,
-    mixed_hbm, cache_hbm,
+    mixed, cache,
     qbuf, kbuf, vbuf, wbuf, kcat, vcat, bias, probs, totals, att,
     zsend, zrecv, own1, xsend, xrecv, x2send, x2recv, own2, z2send, z2recv,
-    mixbuf, cachebuf,
     prompt, rank, length, slot,
     local_sem, send_sem, recv_sem,
 ):
@@ -88,51 +98,50 @@
         sent.append(copy)
         return copy
 
+    bufs = {"k": kbuf, "v": vbuf}
+    copies = {}
+
+    def start_copy(name):
+        if name[0] in "zfx":
+            kind, buf, slot_at = name[0], bufs[name[1]], int(name[2:])
+        else:
+            kind, buf, slot_at = name[2], bufs[name[0]], int(name[1])
+        onward_up = (slot_at < 2) == (buf is kbuf)
+        source, target, count, device = {
+            "z": lambda: {
+                3: (0, 3, 1, z_up),
+                1: (0, 1, 1, z_down),
+                2: (3, 2, 1, z_up) if buf is kbuf else (1, 2, 1, z_down),
+            }[slot_at],
+            "u": lambda: (slot_at, 12 + slot_at, 1, y_up),
+            "d": lambda: (slot_at, 4 + slot_at, 1, y_down),
+            "f": lambda: (12 + slot_at, 8 + slot_at, 1, y_up)
+            if onward_up
+            else (4 + slot_at, 8 + slot_at, 1, y_down),
+            "x": lambda: (
+                slot_at, 16 + slot_at, {0: 1, 1: 3, 4: 4, 12: 4, 8: 2, 10: 2}[slot_at], sibling
+            ),
+        }[kind]()
+        copies[name] = send(
+            buf.at[pl.ds(source, count)], buf.at[pl.ds(target, count)], device
+        )
+
+    arrived = set()
+
+    def arrive(name):
+        if name not in arrived:
+            arrived.add(name)
+            copies[name].wait_recv()
+
     own_k.wait()
     own_v.wait()
-    z_k = {3: send(kbuf.at[0], kbuf.at[3], z_up), 1: send(kbuf.at[0], kbuf.at[1], z_down)}
-    yu, yd = {}, {}
-
-    def along_y(name, buf, dz):
-        yu[name, dz] = send(buf.at[dz], buf.at[12 + dz], y_up)
-        yd[name, dz] = send(buf.at[dz], buf.at[4 + dz], y_down)
-
-    far = {}
-
-    def onward(name, buf, dz):
-        if dz < 2:
-            yu[name, dz].wait_recv()
-            far[name, dz] = send(buf.at[12 + dz], buf.at[8 + dz], y_up)
-        else:
-            yd[name, dz].wait_recv()
-            far[name, dz] = send(buf.at[4 + dz], buf.at[8 + dz], y_down)
-
-    def rest_near(name, dz):
-        (yd if dz < 2 else yu)[name, dz].wait_recv()
-
-    across = {}
-
-    def to_sibling(name, buf, start, count):
-        across[name, start] = send(
-            buf.at[pl.ds(start, count)], buf.at[pl.ds(16 + start, count)], sibling
-        )
-
-    along_y("k", kbuf, 0)
-    z_v = {3: send(vbuf.at[0], vbuf.at[3], z_up), 1: send(vbuf.at[0], vbuf.at[1], z_down)}
-    along_y("v", vbuf, 0)
-    to_sibling("k", kbuf, 0, 1)
-    to_sibling("v", vbuf, 0, 1)
-
-    z_k[3].wait_recv()
-    z_k[2] = send(kbuf.at[3], kbuf.at[2], z_up)
-    along_y("k", kbuf, 3)
-    z_k[1].wait_recv()
-    along_y("k", kbuf, 1)
+    first_head = PLAN.index("#")
+    for step in PLAN[:PLAN.index("?zk3")]:
+        (start_copy if step[0] == "+" else arrive)(step[1:])
 
     for copy in tables:
         copy.wait()
     my_prompt, my_rank, my_len = prompt[me], rank[me], length[me]
-
     who, live = [me] * EARLIER, [jnp.int32(0)] * EARLIER
     for j in range(32):
         same, its_rank, its_len = prompt[j] == my_prompt, rank[j], length[j]
@@ -155,31 +164,8 @@
     for s in range(EARLIER):
         bias[:, s * SPAN:(s + 1) * SPAN] = jnp.where(lane < live[s], 0.0, NEG)
 
-    z_k[2].wait_recv()
-    along_y("k", kbuf, 2)
-    to_sibling("k", kbuf, 1, 3)
-    z_v[3].wait_recv()
-    z_v[1].wait_recv()
-    z_v[2] = send(vbuf.at[1], vbuf.at[2], z_down)
-    onward("k", kbuf, 0)
-    along_y("v", vbuf, 3)
-    along_y("v", vbuf, 1)
-    onward("k", kbuf, 3)
-    onward("k", kbuf, 1)
-    onward("k", kbuf, 2)
-    z_v[2].wait_recv()
-    along_y("v", vbuf, 2)
-    to_sibling("v", vbuf, 1, 3)
-    for dz in range(4):
-        rest_near("k", dz)
-    to_sibling("k", kbuf, 4, 4)
-    to_sibling("k", kbuf, 12, 4)
-    onward("v", vbuf, 0)
-    for dz in range(4):
-        far["k", dz].wait_recv()
-    to_sibling("k", kbuf, 8, 4)
-    for start in (0, 1, 4, 12, 8):
-        across["k", start].wait_recv()
+    for step in PLAN[PLAN.index("?zk3"):first_head]:
+        (start_copy if step[0] == "+" else arrive)(step[1:])
 
     q_copy.wait()
     for s in range(EARLIER):
@@ -212,30 +198,15 @@
             probs[head, pl.ds(start, rows), EARLIER * SPAN:] = here.astype(jnp.bfloat16)
             totals[head, pl.ds(start, rows), :] = jnp.broadcast_to(inverse, (rows, HD))
 
-    def near_done():
-        for dz in range(4):
-            rest_near("v", dz)
-        to_sibling("v", vbuf, 4, 4)
-        to_sibling("v", vbuf, 12, 4)
-
-    def far_done():
-        for dz in range(4):
-            far["v", dz].wait_recv()
-        to_sibling("v", vbuf, 8, 4)
-
-    between = {
-        1: lambda: onward("v", vbuf, 3),
-        2: lambda: onward("v", vbuf, 1),
-        4: lambda: onward("v", vbuf, 2),
-        5: near_done,
-        7: far_done,
-    }
-    for head in range(HEADS):
-        weigh(head)
-        if head in between:
-            between[head]()
-    for start in (0, 1, 4, 12, 8):
-        across["v", start].wait_recv()
+    head = 0
+    for step in PLAN[first_head:]:
+        if step == "#":
+            weigh(head)
+            head += 1
+        else:
+            (start_copy if step[0] == "+" else arrive)(step[1:])
+    for name in copies:
+        arrive(name)
 
     for s in range(EARLIER):
         vcat[s * SPAN:(s + 1) * SPAN, :] = vbuf[place(who[s])]
@@ -286,8 +257,7 @@
         its, second = place(block_of[s] >> 1), (block_of[s] & 1) == 1
         for buf, at in ((kbuf, 0), (vbuf, HD)):
             block = buf[its]
-            cachebuf[s, :, at:at + HD] = jnp.where(second, block[SPAN // 2:], block[:SPAN // 2])
-    cache_copy = local(cachebuf, cache_hbm)
+            cache[s, :, at:at + HD] = jnp.where(second, block[SPAN // 2:], block[:SPAN // 2])
     pass_on(3)
 
     for dx in (1, 3, 2):
@@ -296,8 +266,7 @@
     total = own2[0] + z2recv[...].astype(jnp.float32)
     for k in range(3):
         total = total + x2recv[k, 0].astype(jnp.float32)
-    mixbuf[ZROWS:, :] = total.astype(jnp.bfloat16)
-    out_low = local(mixbuf.at[pl.ds(ZROWS, XROWS)], mixed_hbm.at[pl.ds(ZROWS, XROWS)])
+    mixed[ZROWS:, :] = total.astype(jnp.bfloat16)
 
     z1[0].wait_recv()
     for dx in (2, 1, 3):
@@ -305,14 +274,10 @@
     total = own1[0] + zrecv[0].astype(jnp.float32)
     for k in range(3):
         total = total + xrecv[k].astype(jnp.float32)
-    mixbuf[:ZROWS, :] = total.astype(jnp.bfloat16)
-    out_high = local(mixbuf.at[pl.ds(0, ZROWS)], mixed_hbm.at[pl.ds(0, ZROWS)])
+    mixed[:ZROWS, :] = total.astype(jnp.bfloat16)
 
     for copy in sent:
         copy.wait_send()
-    cache_copy.wait()
-    out_low.wait()
-    out_high.wait()
 
 
 def on_device(queries, key_values, out_weight, prompt_of, cycle_rank, span_len, cache_slot):
@@ -322,11 +287,11 @@
     return pl.pallas_call(
         kernel,
         out_shape=(
-            jax.ShapeDtypeStruct((SPAN, CHUNK), bf16),
-            jax.ShapeDtypeStruct((2, SPAN // 2, 2 * HD), bf16),
+            vmem((SPAN, CHUNK), bf16),
+            vmem((2, SPAN // 2, 2 * HD), bf16),
         ),
         in_specs=[pl.BlockSpec(memory_space=pl.ANY)] * 7,
-        out_specs=[pl.BlockSpec(memory_space=pl.ANY)] * 2,
+        out_specs=(pl.BlockSpec(memory_space=pltpu.VMEM),) * 2,
         scratch_shapes=[
             vmem((SPAN, width), bf16),
             vmem((32, SPAN, HD), bf16),
@@ -348,8 +313,6 @@
             vmem((2, XROWS, CHUNK), f32),
             vmem((XROWS, CHUNK), bf16),
             vmem((XROWS, CHUNK), bf16),
-            vmem((SPAN, CHUNK), bf16),
-            vmem((2, SPAN // 2, 2 * HD), bf16),
             pltpu.SMEM((32,), jnp.int32),
             pltpu.SMEM((32,), jnp.int32),
             pltpu.SMEM((32,), jnp.int32),

time: 67.7 us -> 63.1 us (0.932)
  Pallas kernels: 63.1 us -> 61.1 us
  local copies, waits for them, and re-layouts: 3.24 us -> 1.36 us
    pallas_call x1, Pallas kernels: 63.1 us -> 61.1 us  [on_device(): pl.pallas_call(kernel, out_shape=(vmem((SPAN, CHUNK), bf16), vmem((2, SPA...]
    unnamed x2, local copies, waits for them, and re-layouts: 3.24 us -> 1.36 us
where the time goes in v2:
time: 63.1 us
  Pallas kernels  61.1 us (97%)
  local copies, waits for them, and re-layouts  1.36 us (2%)
  between operations  0.64 us (1%)
    pallas_call x1, Pallas kernels, on_device(): pl.pallas_call(kernel, out_shape=(vmem((SPAN, CHUNK), bf16), vmem((2, SPA...  61.1 us
    unnamed x2, local copies, waits for them, and re-layouts  1.36 us

profile of v2, /device:TPU:1, one launch (start us, length us, event | category | flops | bytes accessed | tf_op | source)
XLA Modules:
  0.0 63.1 jit_solution(12539141436908749676)
XLA Ops:
  0.6 61.1 %shard_map.86 = (bf16[256,512]{1,0:T(8,128)(2,1)S(1)}, bf16[2,128,256]{2,1,0:T(8,128)(2,1)S(1)}) custom-call(bf16[256,1024]{1,0:T(8,128)(2,1)} %q_hbm.1, bf16[256,256]{1,0:T(8,128)(2,1)} %kv_hbm.1, bf16[1024,4096]{1,0:T(8,128)(2,1)} %w_hbm.1, s32[32]{0:T(128)} %prompt_hbm.1, s32[32]{0:T(128)} %rank_hbm.1, s32[32]{0:T(128)} %len_hbm.1, s32[64]{0:T(128)} %slot_hbm.1), custom_call_target="tpu_custom_call" | custom-call | flops 4026531840 | bytes 10485760 | tf_op jit(solution)/shard_map/pallas_call | solution.py:287
  61.7 0.7 %copy.11 = bf16[256,512]{1,0:T(8,128)(2,1)} copy(bf16[256,512]{1,0:T(8,128)(2,1)S(1)} %get-tuple-element.2) | data formatting | bytes 524288
  62.4 0.7 %copy.12 = bf16[2,128,256]{2,1,0:T(8,128)(2,1)} copy(bf16[2,128,256]{2,1,0:T(8,128)(2,1)S(1)} %get-tuple-element.3) | data formatting | bytes 262144

commit v3 on v2

v3 whole, which is shorter than its diff:
```python
import functools
import math

import jax
import jax.numpy as jnp
from jax import lax
from jax.experimental import pallas as pl
from jax.experimental.pallas import tpu as pltpu
from jax.sharding import PartitionSpec as P

HD = 128
SPAN = 256
HEADS = 8
EARLIER = 6
KEYS = (EARLIER + 1) * SPAN
CHUNK = 512
ZROWS = 96
XROWS = SPAN - ZROWS
ZCUT, XCUT = 48, 80
PART = 128
NEG = -1e30
MESH = pl.DeviceIdType.MESH
COPIES = 96

PLAN = (
    "+zk1", "+zk3", "+zk2", "+zv3", "+zv1", "+v0d", "+k0d", "+k0u", "+v0u", "?v0d", "+fv0", "?k0u",
    "+fk0", "?zk1", "?zk3", "+k1u", "+zv2", "?k0d", "+xv0", "+k1d", "+k3u", "+k3d", "?zk2", "+k2d",
    "+k2u", "?v0u", "?k3d", "+fk3", "?k1u", "+xk1", "+fk1", "?zv3", "?fk0", "+v3u", "?k2d", "+fk2",
    "?k3u", "?k1d", "?k2u", "+xk0", "?fv0", "?zv1", "+xk12", "+v1u", "?xk0", "+v1d", "?xk12",
    "?fk3", "?zv2", "?fk1", "+xk8", "+xv1", "?xv0", "+v2u", "+v2d", "+xk4", "?fk2", "+xk10",
    "+v3d", "?v3u", "?xk8", "?xv1", "?xk1", "?v1u", "+fv3", "?xk4", "?xk10", "#", "#", "?v1d", "#",
    "+fv1", "?v2u", "+fv2", "#", "+xv12", "?v2d", "#", "#", "#", "#", "#", "#", "?v3d", "+xv4",
    "#", "#", "?fv3", "?xv12", "?fv1", "+xv8", "?fv2", "+xv10", "#", "#", "#", "#", "?xv4", "?xv8",
    "?xv10",
)

SUM_PLAN = (
    "!pvB", "!B21", "+r1b", "+r1a", "!pvA", "!A11", "!A21", "!A31", "+z12", "!B20", "+r0b", "+z11",
    "!B10", "+r0a", "!B11", "!A00", "!B31", "!B01", "!A20", "?r1b", "!eb1", "+x231", "?r1a",
    "!ea1", "+x211", "?z12", "!p2", "+t2a", "+z13", "?r0a", "!A30", "?r0b", "!B30", "!ea0", "+t2b",
    "!B00", "!A01", "+x210", "+z10", "!eb0", "+x230", "?x231", "?x211", "!q", "+z2", "?z13",
    "?z11", "?t2b", "!A10", "?t2a", "!p1", "+x11", "!p3", "+x13", "?z10", "!cache", "?z2", "?x210",
    "?x230", "!fl", "?x13", "?x11", "!fh",
)


def kernel(
    q_hbm, kv_hbm, w_hbm, prompt_hbm, rank_hbm, len_hbm, slot_hbm,
    mixed, cache,
    qbuf, kbuf, vbuf, wbuf, kcat, vcat, probs, totals, att,
    zsend, zrecv, own1, tsend, trecv, x1send, x1recv,
    rsend, rrecv, own2, x2send, x2recv, z2send, z2recv,
    prompt, rank, length, slot,
    local_sem, send_sem, recv_sem,
):
    me = lax.axis_index("inst")
    tp = lax.axis_index("tp")
    y, zh, core = me // 8, (me // 2) % 4, me % 2
    x, zl = tp // 2, tp % 2

    def inst_at(dy, dz, dc):
        return (((y + dy) % 4) * 4 + (zh + dz) % 4) * 2 + (core + dc) % 2

    def tp_at(dx, dz):
        return ((x + dx) % 4) * 2 + (zl + dz) % 2

    z_up, z_down = (inst_at(0, 1, 0), tp), (inst_at(0, 3, 0), tp)
    z_across = (inst_at(0, 2, 0), tp)
    y_up, y_down = (inst_at(1, 0, 0), tp), (inst_at(3, 0, 0), tp)
    sibling = (inst_at(0, 0, 1), tp)
    z_pair = (me, tp_at(0, 1))
    x_up, x_down = (me, tp_at(1, 0)), (me, tp_at(3, 0))

    n_local = [0]

    def local(src, dst):
        copy = pltpu.make_async_copy(src, dst, local_sem.at[n_local[0]])
        n_local[0] += 1
        copy.start()
        return copy

    own_k = local(kv_hbm.at[:, pl.ds(0, HD)], kbuf.at[0])
    own_v = local(kv_hbm.at[:, pl.ds(HD, HD)], vbuf.at[0])
    tables = [
        local(src, dst)
        for src, dst in (
            (prompt_hbm, prompt), (rank_hbm, rank), (len_hbm, length), (slot_hbm, slot)
        )
    ]
    q_copy = local(q_hbm, qbuf)

    barrier = pltpu.get_barrier_semaphore()
    friends = [z_up, z_down, z_across, y_up, y_down, sibling, z_pair, x_up, x_down]
    for friend in friends:
        pl.semaphore_signal(barrier, inc=1, device_id=friend, device_id_type=MESH)
    w_copies = {}
    for dz in (1, 0):
        for dx in (2, 1, 3, 0):
            columns = pl.ds(pl.multiple_of(tp_at(dx, dz) * CHUNK, CHUNK), CHUNK)
            w_copies[dx, dz] = local(w_hbm.at[:, columns], wbuf.at[dx * 2 + dz])
    pl.semaphore_wait(barrier, len(friends))

    sent = []

    def send(src, dst, device):
        index = len(sent)
        copy = pltpu.make_async_remote_copy(
            src_ref=src, dst_ref=dst, send_sem=send_sem.at[index], recv_sem=recv_sem.at[index],
            device_id=device, device_id_type=MESH,
        )
        copy.start()
        sent.append(copy)
        return copy

    bufs = {"k": kbuf, "v": vbuf}
    copies = {}

    def start_copy(name):
        if name[0] in "zfx":
            kind, buf, slot_at = name[0], bufs[name[1]], int(name[2:])
        else:
            kind, buf, slot_at = name[2], bufs[name[0]], int(name[1])
        onward_up = (slot_at < 2) == (buf is kbuf)
        source, target, count, device = {
            "z": lambda: {
                3: (0, 3, 1, z_up),
                1: (0, 1, 1, z_down),
                2: (0, 2, 1, z_across),
            }[slot_at],
            "u": lambda: (slot_at, 12 + slot_at, 1, y_up),
            "d": lambda: (slot_at, 4 + slot_at, 1, y_down),
            "f": lambda: (12 + slot_at, 8 + slot_at, 1, y_up)
            if onward_up
            else (4 + slot_at, 8 + slot_at, 1, y_down),
            "x": lambda: (
                slot_at, 16 + slot_at, {0: 1, 1: 3, 4: 4, 12: 4, 8: 2, 10: 2}[slot_at], sibling
            ),
        }[kind]()
        copies[name] = send(
            buf.at[pl.ds(source, count)], buf.at[pl.ds(target, count)], device
        )

    arrived = set()

    def arrive(name):
        if name not in arrived:
            arrived.add(name)
            copies[name].wait_recv()

    own_k.wait()
    own_v.wait()
    first_head = PLAN.index("#")
    for step in PLAN[:PLAN.index("?zk1")]:
        (start_copy if step[0] == "+" else arrive)(step[1:])

    for copy in tables:
        copy.wait()
    my_prompt, my_rank, my_len = prompt[me], rank[me], length[me]
    who, live = [me] * EARLIER, [jnp.int32(0)] * EARLIER
    for j in range(32):
        same, its_rank, its_len = prompt[j] == my_prompt, rank[j], length[j]
        for s in range(EARLIER):
            hit = same & (its_rank == s) & (s < my_rank)
            who[s] = jnp.where(hit, j, who[s])
            live[s] = jnp.where(hit, its_len, live[s])
    block_of = [jnp.int32(0)] * 2
    for b in range(64):
        for s in range(2):
            block_of[s] = jnp.where(slot[b] == 2 * me + s, b, block_of[s])

    def place(j):
        dy = ((j >> 3) + 4 - y) & 3
        dz = (((j >> 1) & 3) + 4 - zh) & 3
        dc = ((j & 1) + 2 - core) & 1
        return dc * 16 + dy * 4 + dz

    key_row = lax.broadcasted_iota(jnp.int32, (SPAN, HD), 0)
    first_lane = lax.broadcasted_iota(jnp.int32, (SPAN, HD), 1) == 0
    for s in range(EARLIER):
        dead = first_lane & (key_row >= live[s])
        kcat[s * SPAN:(s + 1) * SPAN, HD:] = jnp.where(dead, NEG, 0.0).astype(jnp.bfloat16)
    kcat[EARLIER * SPAN:, HD:] = jnp.zeros((SPAN, HD), jnp.bfloat16)

    for step in PLAN[PLAN.index("?zk1"):first_head]:
        (start_copy if step[0] == "+" else arrive)(step[1:])

    q_copy.wait()
    for s in range(EARLIER):
        kcat[s * SPAN:(s + 1) * SPAN, :HD] = kbuf[place(who[s])]
    kcat[EARLIER * SPAN:, :HD] = kbuf[0]
    factor = math.log2(math.e) / math.sqrt(HD)

    ones = (lax.broadcasted_iota(jnp.int32, (PART, HD), 1) == 0).astype(jnp.bfloat16)

    def weigh(head, start):
        rows = slice(start, start + PART)
        query = qbuf[rows, head * HD:(head + 1) * HD]
        scores = lax.dot_general(
            jnp.concatenate([query, ones], axis=1), kcat[...],
            (((1,), (1,)), ((), ())), preferred_element_type=jnp.float32,
        )
        earlier = scores[:, :EARLIER * SPAN]
        row = lax.broadcasted_iota(jnp.int32, (PART, SPAN), 0) + start
        column = lax.broadcasted_iota(jnp.int32, (PART, SPAN), 1)
        here = jnp.where(column <= row, scores[:, EARLIER * SPAN:], NEG)
        top = jnp.maximum(
            jnp.max(earlier, axis=1, keepdims=True), jnp.max(here, axis=1, keepdims=True)
        )
        earlier = jnp.exp2((earlier - top) * factor)
        here = jnp.exp2((here - top) * factor)
        total = jnp.sum(earlier, axis=1, keepdims=True) + jnp.sum(here, axis=1, keepdims=True)
        its_row = lax.broadcasted_iota(jnp.int32, (PART, 1), 0) + start
        inverse = jnp.where(its_row < my_len, 1.0 / total, 0.0)
        probs[head, rows, :EARLIER * SPAN] = earlier.astype(jnp.bfloat16)
        probs[head, rows, EARLIER * SPAN:] = here.astype(jnp.bfloat16)
        totals[head, rows, :] = jnp.broadcast_to(inverse, (PART, HD))

    weighed = 0
    for step in PLAN[first_head:]:
        if step == "#":
            weigh(weighed * PART // SPAN, weighed * PART % SPAN)
            weighed += 1
        else:
            (start_copy if step[0] == "+" else arrive)(step[1:])
    for name in copies:
        arrive(name)

    for s in range(EARLIER):
        vcat[s * SPAN:(s + 1) * SPAN, :] = vbuf[place(who[s])]
    vcat[EARLIER * SPAN:, :] = vbuf[0]

    def attend(rows):
        for head in range(HEADS):
            numer = jnp.dot(probs[head, rows, :], vcat[...], preferred_element_type=jnp.float32)
            attended = numer * totals[head, rows, :]
            att[rows, head * HD:(head + 1) * HD] = attended.astype(jnp.bfloat16)

    low, high = slice(0, ZROWS), slice(ZROWS, SPAN)
    ready = set()

    def project(rows, dx, dz):
        if (dx, dz) not in ready:
            ready.add((dx, dz))
            w_copies[dx, dz].wait()
        return jnp.dot(att[rows, :], wbuf[dx * 2 + dz], preferred_element_type=jnp.float32)

    def low_term(dx, dz):
        if dz:
            zsend[dx] = project(low, dx, dz).astype(jnp.bfloat16)
        else:
            own1[dx] = project(low, dx, dz)

    def high_term(dx, dz):
        if dx == 2:
            rsend[dz] = project(high, dx, dz).astype(jnp.bfloat16)
        else:
            own2[dz, {0: 0, 1: 1, 3: 2}[dx]] = project(high, dx, dz)

    def wide(values):
        return values.astype(jnp.float32)

    def pair_sum(dx):
        total = own1[dx] + wide(zrecv[dx])
        if dx == 2:
            tsend[...] = total.astype(jnp.bfloat16)
        elif dx == 1:
            x1send[0, :ZCUT, :] = (total[:ZCUT] + wide(trecv[:ZCUT, :])).astype(jnp.bfloat16)
            x1send[0, ZCUT:, :] = total[ZCUT:].astype(jnp.bfloat16)
        else:
            x1send[1, :ZCUT, :] = total[:ZCUT].astype(jnp.bfloat16)
            x1send[1, ZCUT:, :] = (total[ZCUT:] + wide(trecv[ZCUT:, :])).astype(jnp.bfloat16)

    def up_sum(dz):
        own = own2[dz, 1]
        x2send[dz, 0, :XCUT, :] = (own[:XCUT] + wide(rrecv[dz, :XCUT, :])).astype(jnp.bfloat16)
        x2send[dz, 0, XCUT:, :] = own[XCUT:].astype(jnp.bfloat16)

    def down_sum(dz):
        own = own2[dz, 2]
        x2send[dz, 1, :XCUT, :] = own[:XCUT].astype(jnp.bfloat16)
        x2send[dz, 1, XCUT:, :] = (own[XCUT:] + wide(rrecv[dz, XCUT:, :])).astype(jnp.bfloat16)

    def x_sum(dz):
        return own2[dz, 0] + wide(x2recv[dz, 0]) + wide(x2recv[dz, 1])

    def other_half():
        z2send[...] = x_sum(1).astype(jnp.bfloat16)

    def finish_high():
        mixed[high, :] = (x_sum(0) + wide(z2recv[...])).astype(jnp.bfloat16)

    def finish_low():
        total = own1[0] + wide(zrecv[0]) + wide(x1recv[0]) + wide(x1recv[1])
        mixed[low, :] = total.astype(jnp.bfloat16)

    def decode():
        for s in range(2):
            its, second = place(block_of[s] >> 1), (block_of[s] & 1) == 1
            for buf, at in ((kbuf, 0), (vbuf, HD)):
                block = buf[its]
                cache[s, :, at:at + HD] = jnp.where(second, block[SPAN // 2:], block[:SPAN // 2])

    steps = {
        "pvA": lambda: attend(low), "pvB": lambda: attend(high), "cache": decode,
        "q": other_half, "fl": finish_high, "fh": finish_low,
    }
    routes = {
        "z2": (z2send, z2recv, z_pair),
        "t2a": (tsend.at[pl.ds(0, ZCUT)], trecv.at[pl.ds(0, ZCUT)], x_up),
        "t2b": (
            tsend.at[pl.ds(ZCUT, ZROWS - ZCUT)], trecv.at[pl.ds(ZCUT, ZROWS - ZCUT)], x_down
        ),
        "x11": (x1send.at[0], x1recv.at[0], x_up),
        "x13": (x1send.at[1], x1recv.at[1], x_down),
    }
    for dx in range(4):
        routes[f"z1{dx}"] = (zsend.at[dx], zrecv.at[dx], z_pair)
        for dz in range(2):
            steps[f"A{dx}{dz}"] = functools.partial(low_term, dx, dz)
            steps[f"B{dx}{dz}"] = functools.partial(high_term, dx, dz)
    for dx in (1, 2, 3):
        steps[f"p{dx}"] = functools.partial(pair_sum, dx)
    for dz in range(2):
        steps[f"ea{dz}"] = functools.partial(up_sum, dz)
        steps[f"eb{dz}"] = functools.partial(down_sum, dz)
        for name, start, count, device in (
            (f"r{dz}a", 0, XCUT, x_up), (f"r{dz}b", XCUT, XROWS - XCUT, x_down)
        ):
            rows = pl.ds(start, count)
            routes[name] = (rsend.at[dz, rows], rrecv.at[dz, rows], device)
        routes[f"x21{dz}"] = (x2send.at[dz, 0], x2recv.at[dz, 0], x_up)
        routes[f"x23{dz}"] = (x2send.at[dz, 1], x2recv.at[dz, 1], x_down)
    for step in SUM_PLAN:
        name = step[1:]
        if step[0] == "+":
            copies[name] = send(*routes[name])
        elif step[0] == "?":
            arrive(name)
        else:
            steps[name]()

    for copy in sent:
        copy.wait_send()


def on_device(queries, key_values, out_weight, prompt_of, cycle_rank, span_len, cache_slot):
    bf16, f32 = jnp.bfloat16, jnp.float32
    width = HEADS * HD
    vmem = pltpu.VMEM
    return pl.pallas_call(
        kernel,
        out_shape=(
            vmem((SPAN, CHUNK), bf16),
            vmem((2, SPAN // 2, 2 * HD), bf16),
        ),
        in_specs=[pl.BlockSpec(memory_space=pl.ANY)] * 7,
        out_specs=(pl.BlockSpec(memory_space=pltpu.VMEM),) * 2,
        scratch_shapes=[
            vmem((SPAN, width), bf16),
            vmem((32, SPAN, HD), bf16),
            vmem((32, SPAN, HD), bf16),
            vmem((8, width, CHUNK), bf16),
            vmem((KEYS, 2 * HD), bf16),
            vmem((KEYS, HD), bf16),
            vmem((HEADS, SPAN, KEYS), bf16),
            vmem((HEADS, SPAN, HD), f32),
            vmem((SPAN, width), bf16),
            vmem((4, ZROWS, CHUNK), bf16),
            vmem((4, ZROWS, CHUNK), bf16),
            vmem((4, ZROWS, CHUNK), f32),
            vmem((ZROWS, CHUNK), bf16),
            vmem((ZROWS, CHUNK), bf16),
            vmem((2, ZROWS, CHUNK), bf16),
            vmem((2, ZROWS, CHUNK), bf16),
            vmem((2, XROWS, CHUNK), bf16),
            vmem((2, XROWS, CHUNK), bf16),
            vmem((2, 3, XROWS, CHUNK), f32),
            vmem((2, 2, XROWS, CHUNK), bf16),
            vmem((2, 2, XROWS, CHUNK), bf16),
            vmem((XROWS, CHUNK), bf16),
            vmem((XROWS, CHUNK), bf16),
            pltpu.SMEM((32,), jnp.int32),
            pltpu.SMEM((32,), jnp.int32),
            pltpu.SMEM((32,), jnp.int32),
            pltpu.SMEM((64,), jnp.int32),
            pltpu.SemaphoreType.DMA((24,)),
            pltpu.SemaphoreType.DMA((COPIES,)),
            pltpu.SemaphoreType.DMA((COPIES,)),
        ],
        compiler_params=pltpu.CompilerParams(
            collective_id=0, has_side_effects=True, vmem_limit_bytes=56 * 1024 * 1024
        ),
        cost_estimate=pl.CostEstimate(
            flops=4 * SPAN * HEADS * KEYS * HD + 2 * SPAN * width * 4096,
            bytes_accessed=10 * 1024 * 1024,
            transcendentals=HEADS * SPAN * KEYS,
        ),
    )(queries, key_values, out_weight, prompt_of, cycle_rank, span_len, cache_slot)


def solution(mesh):
    placed = (P("inst", "tp"), P("inst", "tp"), P("tp", None), P(), P(), P(), P())
    return jax.shard_map(
        on_device,
        mesh=mesh,
        in_specs=placed,
        out_specs=(P("inst", "tp"), P("inst", None, "tp")),
        check_vma=False,
    )
```

time: 63.1 us -> 58.4 us (0.926)
  Pallas kernels: 61.1 us -> 56.3 us
    pallas_call x1, Pallas kernels: 61.1 us -> 56.3 us  [on_device(): pl.pallas_call(kernel, out_shape=(vmem((SPAN, CHUNK), bf16), vmem((2, SPA...]
where the time goes in v3:
time: 58.4 us; the launch traced here: 58.3 us
  Pallas kernels  56.3 us (96%)
  local copies, waits for them, and re-layouts  1.36 us (2%)
  between operations  0.64 us (1%)
    pallas_call x1, Pallas kernels, on_device(): pl.pallas_call(kernel, out_shape=(vmem((SPAN, CHUNK), bf16), vmem((2, SPA...  56.3 us
    unnamed x2, local copies, waits for them, and re-layouts  1.36 us

profile of v3, /device:TPU:1, one launch (start us, length us, event | category | flops | bytes accessed | tf_op | source)
XLA Modules:
  0.0 58.3 jit_solution(6848662253949336420)
XLA Ops:
  0.6 56.3 %shard_map.86 = (bf16[256,512]{1,0:T(8,128)(2,1)S(1)}, bf16[2,128,256]{2,1,0:T(8,128)(2,1)S(1)}) custom-call(bf16[256,1024]{1,0:T(8,128)(2,1)} %q_hbm.1, bf16[256,256]{1,0:T(8,128)(2,1)} %kv_hbm.1, bf16[1024,4096]{1,0:T(8,128)(2,1)} %w_hbm.1, s32[32]{0:T(128)} %prompt_hbm.1, s32[32]{0:T(128)} %rank_hbm.1, s32[32]{0:T(128)} %len_hbm.1, s32[64]{0:T(128)} %slot_hbm.1), custom_call_target="tpu_custom_call" | custom-call | flops 4026531840 | bytes 10485760 | tf_op jit(solution)/shard_map/pallas_call | solution.py:350
  57.0 0.7 %copy.11 = bf16[256,512]{1,0:T(8,128)(2,1)} copy(bf16[256,512]{1,0:T(8,128)(2,1)S(1)} %get-tuple-element.2) | data formatting | bytes 524288
  57.7 0.7 %copy.12 = bf16[2,128,256]{2,1,0:T(8,128)(2,1)} copy(bf16[2,128,256]{2,1,0:T(8,128)(2,1)S(1)} %get-tuple-element.3) | data formatting | bytes 262144

commit v4 on v3

--- a/solution.py
+++ b/solution.py
@@ -14,33 +14,39 @@
 EARLIER = 6
 KEYS = (EARLIER + 1) * SPAN
 CHUNK = 512
-ZROWS = 96
+ZROWS = 112
 XROWS = SPAN - ZROWS
-ZCUT, XCUT = 48, 80
-PART = 128
+ZCUT, XCUT = 48, 64
+PART = SPAN
 NEG = -1e30
 MESH = pl.DeviceIdType.MESH
-COPIES = 96
+COPIES = 128
+PIECES = ((0, 0, 128), (0, 128, 128), (1, 0, 128), (1, 128, 128))
+SIBLING_FAR = 4
 
 PLAN = (
-    "+zk1", "+zk3", "+zk2", "+zv3", "+zv1", "+v0d", "+k0d", "+k0u", "+v0u", "?v0d", "+fv0", "?k0u",
-    "+fk0", "?zk1", "?zk3", "+k1u", "+zv2", "?k0d", "+xv0", "+k1d", "+k3u", "+k3d", "?zk2", "+k2d",
-    "+k2u", "?v0u", "?k3d", "+fk3", "?k1u", "+xk1", "+fk1", "?zv3", "?fk0", "+v3u", "?k2d", "+fk2",
-    "?k3u", "?k1d", "?k2u", "+xk0", "?fv0", "?zv1", "+xk12", "+v1u", "?xk0", "+v1d", "?xk12",
-    "?fk3", "?zv2", "?fk1", "+xk8", "+xv1", "?xv0", "+v2u", "+v2d", "+xk4", "?fk2", "+xk10",
-    "+v3d", "?v3u", "?xk8", "?xv1", "?xk1", "?v1u", "+fv3", "?xk4", "?xk10", "#", "#", "?v1d", "#",
-    "+fv1", "?v2u", "+fv2", "#", "+xv12", "?v2d", "#", "#", "#", "#", "#", "#", "?v3d", "+xv4",
-    "#", "#", "?fv3", "?xv12", "?fv1", "+xv8", "?fv2", "+xv10", "#", "#", "#", "#", "?xv4", "?xv8",
-    "?xv10",
+    10301, 14300, 14000, 10003, 10203, 14200, 15100, 15300, 19100, 10101, 10103, 10001, 15000,
+    15200, 0, 14100, 25100, 24000, 17100, 24300, 16000, 20301, 12302, 14301, 20003, 15003, 11002,
+    16300, 14003, 15301, 20101, 15101, 12102, 20203, 11202, 14101, 14203, 15203, 20001, 15001,
+    19000, 27100, 14001, 20103, 25003, 10303, 14103, 15103, 10201, 17003, 24301, 22302, 14302,
+    19300, 21002, 15002, 19001, 25101, 14002, 17101, 22102, 14102, 15302, 24001, 25000, 26300,
+    21202, 25200, 25301, 14202, 24200, 15102, 15202, 16001, 24003, 24203, 25002, 20303, 15303,
+    24103, 17002, 16103, 25001, 19200, 26000, 20201, 14303, 24102, 16102, 19301, 19101, 16301,
+    24002, 29100, 14201, 24101, 15201, 25102, 19004, 19201, 25302, 24302, 17200, 25103, 26001,
+    29000, 27101, 27003, 25202, 17302, 25300, 19104, 26103, 19012, 24100, 16203, 25303, 29101,
+    17303, 24202, 19304, 27002, 19112, 16202, 19008, 25203, 24303, 26102, 19108, 29301, 25201,
+    17201, 26301, 29200, 27302, 29304, 29104, 19204, 29012, 24201, 29112, 29300, 29201, 19312,
+    29004, 27200, 29008, 19212, 29001, 26203, 27303, 19308, 29108, 1, 1, 26202, 1, 27201, 19208, 1,
+    1, 1, 1, 29312, 29212, 29204, 29308, 1, 29208,
 )
 
 SUM_PLAN = (
-    "!pvB", "!B21", "+r1b", "+r1a", "!pvA", "!A11", "!A21", "!A31", "+z12", "!B20", "+r0b", "+z11",
-    "!B10", "+r0a", "!B11", "!A00", "!B31", "!B01", "!A20", "?r1b", "!eb1", "+x231", "?r1a",
-    "!ea1", "+x211", "?z12", "!p2", "+t2a", "+z13", "?r0a", "!A30", "?r0b", "!B30", "!ea0", "+t2b",
-    "!B00", "!A01", "+x210", "+z10", "!eb0", "+x230", "?x231", "?x211", "!q", "+z2", "?z13",
-    "?z11", "?t2b", "!A10", "?t2a", "!p1", "+x11", "!p3", "+x13", "?z10", "!cache", "?z2", "?x210",
-    "?x230", "!fl", "?x13", "?x11", "!fh",
+    "!pvB", "!B21", "+r1b", "+r1a", "!pvA", "!A21", "+z12", "!B20", "+r0b", "!B10", "!B30", "!B31",
+    "+r0a", "!A01", "!B11", "!A11", "+z11", "!A31", "?r1a", "!ea1", "+x211", "+z13", "?r1b",
+    "!eb1", "+x231", "!A20", "?z12", "!p2", "!B01", "?r0b", "+t2a", "!eb0", "?r0a", "!A10", "!A30",
+    "+t2b", "!ea0", "+x230", "+x210", "+z10", "!B00", "?x231", "?x211", "!q", "?t2a", "!A00",
+    "+z2", "?z11", "?t2b", "!p1", "?z13", "+x11", "!p3", "+x13", "?x210", "!cache", "?x11", "?z10",
+    "?x230", "?z2", "!fl", "?x13", "!fh",
 )
 
 
@@ -65,7 +71,7 @@
         return ((x + dx) % 4) * 2 + (zl + dz) % 2
 
     z_up, z_down = (inst_at(0, 1, 0), tp), (inst_at(0, 3, 0), tp)
-    z_across = (inst_at(0, 2, 0), tp)
+    z_across, y_across = (inst_at(0, 2, 0), tp), (inst_at(2, 0, 0), tp)
     y_up, y_down = (inst_at(1, 0, 0), tp), (inst_at(3, 0, 0), tp)
     sibling = (inst_at(0, 0, 1), tp)
     z_pair = (me, tp_at(0, 1))
@@ -90,7 +96,7 @@
     q_copy = local(q_hbm, qbuf)
 
     barrier = pltpu.get_barrier_semaphore()
-    friends = [z_up, z_down, z_across, y_up, y_down, sibling, z_pair, x_up, x_down]
+    friends = [z_up, z_down, y_up, y_down, sibling, z_pair, x_up, x_down]
     for friend in friends:
         pl.semaphore_signal(barrier, inc=1, device_id=friend, device_id_type=MESH)
     w_copies = {}
@@ -112,32 +118,22 @@
         sent.append(copy)
         return copy
 
-    bufs = {"k": kbuf, "v": vbuf}
     copies = {}
 
-    def start_copy(name):
-        if name[0] in "zfx":
-            kind, buf, slot_at = name[0], bufs[name[1]], int(name[2:])
-        else:
-            kind, buf, slot_at = name[2], bufs[name[0]], int(name[1])
-        onward_up = (slot_at < 2) == (buf is kbuf)
-        source, target, count, device = {
-            "z": lambda: {
-                3: (0, 3, 1, z_up),
-                1: (0, 1, 1, z_down),
-                2: (0, 2, 1, z_across),
-            }[slot_at],
-            "u": lambda: (slot_at, 12 + slot_at, 1, y_up),
-            "d": lambda: (slot_at, 4 + slot_at, 1, y_down),
-            "f": lambda: (12 + slot_at, 8 + slot_at, 1, y_up)
-            if onward_up
-            else (4 + slot_at, 8 + slot_at, 1, y_down),
-            "x": lambda: (
-                slot_at, 16 + slot_at, {0: 1, 1: 3, 4: 4, 12: 4, 8: 2, 10: 2}[slot_at], sibling
-            ),
-        }[kind]()
-        copies[name] = send(
-            buf.at[pl.ds(source, count)], buf.at[pl.ds(target, count)], device
+    def start_copy(code):
+        kind, piece, at = code // 1000, code // 100 % 10, code % 100
+        which, first_row, rows = PIECES[piece]
+        source, target, device = (
+            (0, at, z_up if at == 3 else z_down),
+            (3, at, z_up), (1, at, z_down), (0, at, z_across),
+            (at, 12 + at, y_up), (at, 4 + at, y_down),
+            (12 + at, 8 + at, y_up), (4 + at, 8 + at, y_down), (at, 8 + at, y_across),
+            (at, 16 + at, sibling),
+        )[kind]
+        count = {0: 1, 1: 3, 4: 4, 12: 4, 8: SIBLING_FAR, 10: 2}[at] if kind == 9 else 1
+        buf, piece_rows = (kbuf, vbuf)[which], pl.ds(first_row, rows)
+        copies[code] = send(
+            buf.at[pl.ds(source, count), piece_rows], buf.at[pl.ds(target, count), piece_rows], device
         )
 
     arrived = set()
@@ -149,24 +145,30 @@
 
     own_k.wait()
     own_v.wait()
-    first_head = PLAN.index("#")
-    for step in PLAN[:PLAN.index("?zk1")]:
-        (start_copy if step[0] == "+" else arrive)(step[1:])
-
-    for copy in tables:
-        copy.wait()
-    my_prompt, my_rank, my_len = prompt[me], rank[me], length[me]
-    who, live = [me] * EARLIER, [jnp.int32(0)] * EARLIER
-    for j in range(32):
-        same, its_rank, its_len = prompt[j] == my_prompt, rank[j], length[j]
+    needs = {}
+
+    def look_up():
+        for copy in tables:
+            copy.wait()
+        my_prompt, my_rank, my_len = prompt[me], rank[me], length[me]
+        who, live = [me] * EARLIER, [jnp.int32(0)] * EARLIER
+        for j in range(32):
+            same, its_rank, its_len = prompt[j] == my_prompt, rank[j], length[j]
+            for s in range(EARLIER):
+                hit = same & (its_rank == s) & (s < my_rank)
+                who[s] = jnp.where(hit, j, who[s])
+                live[s] = jnp.where(hit, its_len, live[s])
+        block_of = [jnp.int32(0)] * 2
+        for b in range(64):
+            for s in range(2):
+                block_of[s] = jnp.where(slot[b] == 2 * me + s, b, block_of[s])
+        needs.update(who=who, block_of=block_of, my_len=my_len)
+        key_row = lax.broadcasted_iota(jnp.int32, (SPAN, HD), 0)
+        first_lane = lax.broadcasted_iota(jnp.int32, (SPAN, HD), 1) == 0
         for s in range(EARLIER):
-            hit = same & (its_rank == s) & (s < my_rank)
-            who[s] = jnp.where(hit, j, who[s])
-            live[s] = jnp.where(hit, its_len, live[s])
-    block_of = [jnp.int32(0)] * 2
-    for b in range(64):
-        for s in range(2):
-            block_of[s] = jnp.where(slot[b] == 2 * me + s, b, block_of[s])
+            dead = first_lane & (key_row >= live[s])
+            kcat[s * SPAN:(s + 1) * SPAN, HD:] = jnp.where(dead, NEG, 0.0).astype(jnp.bfloat16)
+        kcat[EARLIER * SPAN:, HD:] = jnp.zeros((SPAN, HD), jnp.bfloat16)
 
     def place(j):
         dy = ((j >> 3) + 4 - y) & 3
@@ -174,20 +176,12 @@
         dc = ((j & 1) + 2 - core) & 1
         return dc * 16 + dy * 4 + dz
 
-    key_row = lax.broadcasted_iota(jnp.int32, (SPAN, HD), 0)
-    first_lane = lax.broadcasted_iota(jnp.int32, (SPAN, HD), 1) == 0
-    for s in range(EARLIER):
-        dead = first_lane & (key_row >= live[s])
-        kcat[s * SPAN:(s + 1) * SPAN, HD:] = jnp.where(dead, NEG, 0.0).astype(jnp.bfloat16)
-    kcat[EARLIER * SPAN:, HD:] = jnp.zeros((SPAN, HD), jnp.bfloat16)
-
-    for step in PLAN[PLAN.index("?zk1"):first_head]:
-        (start_copy if step[0] == "+" else arrive)(step[1:])
-
-    q_copy.wait()
-    for s in range(EARLIER):
-        kcat[s * SPAN:(s + 1) * SPAN, :HD] = kbuf[place(who[s])]
-    kcat[EARLIER * SPAN:, :HD] = kbuf[0]
+    def take_keys():
+        q_copy.wait()
+        for s in range(EARLIER):
+            kcat[s * SPAN:(s + 1) * SPAN, :HD] = kbuf[place(needs["who"][s])]
+        kcat[EARLIER * SPAN:, :HD] = kbuf[0]
+
     factor = math.log2(math.e) / math.sqrt(HD)
 
     ones = (lax.broadcasted_iota(jnp.int32, (PART, HD), 1) == 0).astype(jnp.bfloat16)
@@ -210,23 +204,29 @@
         here = jnp.exp2((here - top) * factor)
         total = jnp.sum(earlier, axis=1, keepdims=True) + jnp.sum(here, axis=1, keepdims=True)
         its_row = lax.broadcasted_iota(jnp.int32, (PART, 1), 0) + start
-        inverse = jnp.where(its_row < my_len, 1.0 / total, 0.0)
+        inverse = jnp.where(its_row < needs["my_len"], 1.0 / total, 0.0)
         probs[head, rows, :EARLIER * SPAN] = earlier.astype(jnp.bfloat16)
         probs[head, rows, EARLIER * SPAN:] = here.astype(jnp.bfloat16)
         totals[head, rows, :] = jnp.broadcast_to(inverse, (PART, HD))
 
     weighed = 0
-    for step in PLAN[first_head:]:
-        if step == "#":
-            weigh(weighed * PART // SPAN, weighed * PART % SPAN)
+    for step in PLAN:
+        if step == 0:
+            look_up()
+        elif step == 1:
+            if not weighed:
+                take_keys()
+            weigh(weighed, 0)
             weighed += 1
+        elif step < 20000:
+            start_copy(step - 10000)
         else:
-            (start_copy if step[0] == "+" else arrive)(step[1:])
+            arrive(step - 20000)
     for name in copies:
         arrive(name)
 
     for s in range(EARLIER):
-        vcat[s * SPAN:(s + 1) * SPAN, :] = vbuf[place(who[s])]
+        vcat[s * SPAN:(s + 1) * SPAN, :] = vbuf[place(needs["who"][s])]
     vcat[EARLIER * SPAN:, :] = vbuf[0]
 
     def attend(rows):
@@ -295,7 +295,7 @@
 
     def decode():
         for s in range(2):
-            its, second = place(block_of[s] >> 1), (block_of[s] & 1) == 1
+            its, second = place(needs["block_of"][s] >> 1), (needs["block_of"][s] & 1) == 1
             for buf, at in ((kbuf, 0), (vbuf, HD)):
                 block = buf[its]
                 cache[s, :, at:at + HD] = jnp.where(second, block[SPAN // 2:], block[:SPAN // 2])

time: 58.4 us -> 55.6 us (0.952)
  Pallas kernels: 56.3 us -> 53.5 us
    pallas_call x1, Pallas kernels: 56.3 us -> 53.5 us  [on_device(): pl.pallas_call(kernel, out_shape=(vmem((SPAN, CHUNK), bf16), vmem((2, SPA...]
where the time goes in v4:
time: 55.6 us; the launch traced here: 55.5 us
  Pallas kernels  53.5 us (96%)
  local copies, waits for them, and re-layouts  1.36 us (2%)
  between operations  0.64 us (1%)
    pallas_call x1, Pallas kernels, on_device(): pl.pallas_call(kernel, out_shape=(vmem((SPAN, CHUNK), bf16), vmem((2, SPA...  53.5 us
    unnamed x2, local copies, waits for them, and re-layouts  1.36 us

profile of v4, /device:TPU:1, one launch (start us, length us, event | category | flops | bytes accessed | tf_op | source)
XLA Modules:
  0.0 55.5 jit_solution(13277402398764517578)
XLA Ops:
  0.6 53.5 %shard_map.86 = (bf16[256,512]{1,0:T(8,128)(2,1)S(1)}, bf16[2,128,256]{2,1,0:T(8,128)(2,1)S(1)}) custom-call(bf16[256,1024]{1,0:T(8,128)(2,1)} %q_hbm.1, bf16[256,256]{1,0:T(8,128)(2,1)} %kv_hbm.1, bf16[1024,4096]{1,0:T(8,128)(2,1)} %w_hbm.1, s32[32]{0:T(128)} %prompt_hbm.1, s32[32]{0:T(128)} %rank_hbm.1, s32[32]{0:T(128)} %len_hbm.1, s32[64]{0:T(128)} %slot_hbm.1), custom_call_target="tpu_custom_call" | custom-call | flops 4026531840 | bytes 10485760 | tf_op jit(solution)/shard_map/pallas_call | solution.py:350
  54.2 0.7 %copy.11 = bf16[256,512]{1,0:T(8,128)(2,1)} copy(bf16[256,512]{1,0:T(8,128)(2,1)S(1)} %get-tuple-element.2) | data formatting | bytes 524288
  54.9 0.7 %copy.12 = bf16[2,128,256]{2,1,0:T(8,128)(2,1)} copy(bf16[2,128,256]{2,1,0:T(8,128)(2,1)S(1)} %get-tuple-element.3) | data formatting | bytes 262144

commit v5 on v4

--- a/solution.py
+++ b/solution.py
@@ -25,19 +25,19 @@
 SIBLING_FAR = 4
 
 PLAN = (
-    10301, 14300, 14000, 10003, 10203, 14200, 15100, 15300, 19100, 10101, 10103, 10001, 15000,
-    15200, 0, 14100, 25100, 24000, 17100, 24300, 16000, 20301, 12302, 14301, 20003, 15003, 11002,
-    16300, 14003, 15301, 20101, 15101, 12102, 20203, 11202, 14101, 14203, 15203, 20001, 15001,
-    19000, 27100, 14001, 20103, 25003, 10303, 14103, 15103, 10201, 17003, 24301, 22302, 14302,
-    19300, 21002, 15002, 19001, 25101, 14002, 17101, 22102, 14102, 15302, 24001, 25000, 26300,
-    21202, 25200, 25301, 14202, 24200, 15102, 15202, 16001, 24003, 24203, 25002, 20303, 15303,
-    24103, 17002, 16103, 25001, 19200, 26000, 20201, 14303, 24102, 16102, 19301, 19101, 16301,
-    24002, 29100, 14201, 24101, 15201, 25102, 19004, 19201, 25302, 24302, 17200, 25103, 26001,
-    29000, 27101, 27003, 25202, 17302, 25300, 19104, 26103, 19012, 24100, 16203, 25303, 29101,
-    17303, 24202, 19304, 27002, 19112, 16202, 19008, 25203, 24303, 26102, 19108, 29301, 25201,
-    17201, 26301, 29200, 27302, 29304, 29104, 19204, 29012, 24201, 29112, 29300, 29201, 19312,
-    29004, 27200, 29008, 19212, 29001, 26203, 27303, 19308, 29108, 1, 1, 26202, 1, 27201, 19208, 1,
-    1, 1, 1, 29312, 29212, 29204, 29308, 1, 29208,
+    10003, 10101, 14200, 19100, 15100, 14300, 14000, 10001, 10203, 10103, 15200, 14100, 15300,
+    15000, 10301, 25100, 17100, 19300, 25200, 17200, 24300, 16300, 20003, 11002, 20101, 14003,
+    12102, 15003, 10303, 15101, 14101, 10201, 20203, 15203, 14203, 19000, 20001, 15001, 14001,
+    24000, 16000, 20103, 11202, 15103, 25003, 20301, 15301, 12302, 14103, 14301, 17003, 24003,
+    25101, 22102, 14102, 21002, 15002, 14002, 24001, 15102, 25001, 20303, 16001, 24100, 27200,
+    19200, 25000, 15303, 24103, 17101, 29100, 16103, 20201, 21202, 14202, 19001, 15201, 24102,
+    25002, 25203, 24301, 16102, 24101, 19112, 14201, 17002, 22302, 27100, 15302, 14302, 19004,
+    14303, 0, 26300, 15202, 25303, 25102, 25103, 29001, 26001, 19101, 24002, 25301, 26103, 29300,
+    29000, 19012, 19104, 19201, 24200, 17303, 29200, 24203, 27003, 29004, 19301, 24202, 25300,
+    16202, 16203, 27101, 29112, 26000, 25201, 17201, 26102, 19108, 16301, 27002, 19008, 25302,
+    17302, 25202, 29104, 19204, 19304, 24201, 24303, 24302, 29108, 29012, 29101, 29201, 19212,
+    19312, 29301, 29008, 1, 1, 27303, 26203, 27201, 26202, 19208, 1, 27302, 29204, 26301, 19308,
+    29304, 1, 29212, 1, 29312, 1, 1, 1, 29208, 29308,
 )
 
 SUM_PLAN = (

time: 55.6 us -> 55.2 us (level)
  no operation moved by 1% of the time
where the time goes in v5:
time: 55.2 us; the launch traced here: 55.1 us
  Pallas kernels  53.1 us (96%)
  local copies, waits for them, and re-layouts  1.36 us (2%)
  between operations  0.64 us (1%)
    pallas_call x1, Pallas kernels, on_device(): pl.pallas_call(kernel, out_shape=(vmem((SPAN, CHUNK), bf16), vmem((2, SPA...  53.1 us
    unnamed x2, local copies, waits for them, and re-layouts  1.36 us

profile of v5, /device:TPU:1, one launch (start us, length us, event | category | flops | bytes accessed | tf_op | source)
XLA Modules:
  0.0 55.1 jit_solution(17543840266899881690)
XLA Ops:
  0.6 53.1 %shard_map.86 = (bf16[256,512]{1,0:T(8,128)(2,1)S(1)}, bf16[2,128,256]{2,1,0:T(8,128)(2,1)S(1)}) custom-call(bf16[256,1024]{1,0:T(8,128)(2,1)} %q_hbm.1, bf16[256,256]{1,0:T(8,128)(2,1)} %kv_hbm.1, bf16[1024,4096]{1,0:T(8,128)(2,1)} %w_hbm.1, s32[32]{0:T(128)} %prompt_hbm.1, s32[32]{0:T(128)} %rank_hbm.1, s32[32]{0:T(128)} %len_hbm.1, s32[64]{0:T(128)} %slot_hbm.1), custom_call_target="tpu_custom_call" | custom-call | flops 4026531840 | bytes 10485760 | tf_op jit(solution)/shard_map/pallas_call | solution.py:350
  53.7 0.7 %copy.11 = bf16[256,512]{1,0:T(8,128)(2,1)} copy(bf16[256,512]{1,0:T(8,128)(2,1)S(1)} %get-tuple-element.2) | data formatting | bytes 524288
  54.4 0.7 %copy.12 = bf16[2,128,256]{2,1,0:T(8,128)(2,1)} copy(bf16[2,128,256]{2,1,0:T(8,128)(2,1)S(1)} %get-tuple-element.3) | data formatting | bytes 262144

commit v6 on v5

--- a/solution.py
+++ b/solution.py
@@ -25,19 +25,19 @@
 SIBLING_FAR = 4
 
 PLAN = (
-    10003, 10101, 14200, 19100, 15100, 14300, 14000, 10001, 10203, 10103, 15200, 14100, 15300,
-    15000, 10301, 25100, 17100, 19300, 25200, 17200, 24300, 16300, 20003, 11002, 20101, 14003,
-    12102, 15003, 10303, 15101, 14101, 10201, 20203, 15203, 14203, 19000, 20001, 15001, 14001,
-    24000, 16000, 20103, 11202, 15103, 25003, 20301, 15301, 12302, 14103, 14301, 17003, 24003,
-    25101, 22102, 14102, 21002, 15002, 14002, 24001, 15102, 25001, 20303, 16001, 24100, 27200,
-    19200, 25000, 15303, 24103, 17101, 29100, 16103, 20201, 21202, 14202, 19001, 15201, 24102,
-    25002, 25203, 24301, 16102, 24101, 19112, 14201, 17002, 22302, 27100, 15302, 14302, 19004,
-    14303, 0, 26300, 15202, 25303, 25102, 25103, 29001, 26001, 19101, 24002, 25301, 26103, 29300,
-    29000, 19012, 19104, 19201, 24200, 17303, 29200, 24203, 27003, 29004, 19301, 24202, 25300,
-    16202, 16203, 27101, 29112, 26000, 25201, 17201, 26102, 19108, 16301, 27002, 19008, 25302,
-    17302, 25202, 29104, 19204, 19304, 24201, 24303, 24302, 29108, 29012, 29101, 29201, 19212,
-    19312, 29301, 29008, 1, 1, 27303, 26203, 27201, 26202, 19208, 1, 27302, 29204, 26301, 19308,
-    29304, 1, 29212, 1, 29312, 1, 1, 1, 29208, 29308,
+    10003, 14300, 10103, 10101, 10203, 15200, 15100, 15300, 15000, 14000, 10001, 14200, 19100,
+    14100, 10301, 25200, 17200, 24300, 16300, 25100, 17100, 24000, 16000, 20003, 11002, 20101,
+    15003, 12102, 10201, 14101, 14003, 15101, 20001, 20103, 10303, 14001, 15103, 15001, 14103,
+    20203, 20301, 11202, 15203, 14203, 15301, 12302, 27100, 14301, 21002, 15002, 22102, 14102,
+    15102, 25001, 14002, 25000, 26300, 25101, 20201, 15201, 24103, 19200, 20303, 24001, 16103,
+    16001, 14201, 15303, 21202, 26000, 22302, 14202, 15302, 24100, 19201, 17101, 24003, 24102,
+    16102, 25102, 25301, 24200, 19000, 19300, 14303, 19101, 25300, 25003, 24301, 16301, 25103,
+    24203, 17003, 25002, 29100, 19301, 16203, 24002, 17002, 19104, 15202, 25303, 19001, 29201,
+    24101, 17303, 25302, 19304, 14302, 26001, 26103, 17302, 25201, 0, 27101, 27200, 24202, 19012,
+    19112, 17201, 19004, 26102, 16202, 19108, 25203, 29301, 27003, 27002, 19008, 29200, 24201,
+    19212, 29012, 29000, 29304, 29001, 24302, 29300, 27302, 26301, 26203, 27303, 25202, 29004,
+    24303, 19204, 29112, 29108, 29104, 29101, 19312, 19308, 29008, 1, 27201, 26202, 19208, 1, 1, 1,
+    1, 1, 1, 1, 29308, 29204, 29212, 29208, 29312,
 )
 
 SUM_PLAN = (
@@ -77,6 +77,11 @@
     z_pair = (me, tp_at(0, 1))
     x_up, x_down = (me, tp_at(1, 0)), (me, tp_at(3, 0))
 
+    barrier = pltpu.get_barrier_semaphore()
+    friends = [z_up, z_down, y_up, y_down, sibling, z_pair, x_up, x_down]
+    for friend in friends:
+        pl.semaphore_signal(barrier, inc=1, device_id=friend, device_id_type=MESH)
+
     n_local = [0]
 
     def local(src, dst):
@@ -93,17 +98,15 @@
             (prompt_hbm, prompt), (rank_hbm, rank), (len_hbm, length), (slot_hbm, slot)
         )
     ]
-    q_copy = local(q_hbm, qbuf)
-
-    barrier = pltpu.get_barrier_semaphore()
-    friends = [z_up, z_down, y_up, y_down, sibling, z_pair, x_up, x_down]
-    for friend in friends:
-        pl.semaphore_signal(barrier, inc=1, device_id=friend, device_id_type=MESH)
-    w_copies = {}
-    for dz in (1, 0):
-        for dx in (2, 1, 3, 0):
-            columns = pl.ds(pl.multiple_of(tp_at(dx, dz) * CHUNK, CHUNK), CHUNK)
-            w_copies[dx, dz] = local(w_hbm.at[:, columns], wbuf.at[dx * 2 + dz])
+    w_copies, q_copies = {}, []
+
+    def start_large():
+        q_copies.append(local(q_hbm, qbuf))
+        for dz in (1, 0):
+            for dx in (2, 1, 3, 0):
+                columns = pl.ds(pl.multiple_of(tp_at(dx, dz) * CHUNK, CHUNK), CHUNK)
+                w_copies[dx, dz] = local(w_hbm.at[:, columns], wbuf.at[dx * 2 + dz])
+
     pl.semaphore_wait(barrier, len(friends))
 
     sent = []
@@ -177,7 +180,7 @@
         return dc * 16 + dy * 4 + dz
 
     def take_keys():
-        q_copy.wait()
+        q_copies[0].wait()
         for s in range(EARLIER):
             kcat[s * SPAN:(s + 1) * SPAN, :HD] = kbuf[place(needs["who"][s])]
         kcat[EARLIER * SPAN:, :HD] = kbuf[0]
@@ -211,6 +214,8 @@
 
     weighed = 0
     for step in PLAN:
+        if step >= 20000 and not q_copies:
+            start_large()
         if step == 0:
             look_up()
         elif step == 1:

time: 55.2 us -> 55.4 us (level)
  no operation moved by 1% of the time
where the time goes in v6:
time: 55.4 us; the launch traced here: 55.3 us
  Pallas kernels  53.3 us (96%)
  local copies, waits for them, and re-layouts  1.36 us (2%)
  between operations  0.64 us (1%)
    pallas_call x1, Pallas kernels, on_device(): pl.pallas_call(kernel, out_shape=(vmem((SPAN, CHUNK), bf16), vmem((2, SPA...  53.3 us
    unnamed x2, local copies, waits for them, and re-layouts  1.36 us

profile of v6, /device:TPU:1, one launch (start us, length us, event | category | flops | bytes accessed | tf_op | source)
XLA Modules:
  0.0 55.3 jit_solution(18337847774618488411)
XLA Ops:
  0.6 53.3 %shard_map.86 = (bf16[256,512]{1,0:T(8,128)(2,1)S(1)}, bf16[2,128,256]{2,1,0:T(8,128)(2,1)S(1)}) custom-call(bf16[256,1024]{1,0:T(8,128)(2,1)} %q_hbm.1, bf16[256,256]{1,0:T(8,128)(2,1)} %kv_hbm.1, bf16[1024,4096]{1,0:T(8,128)(2,1)} %w_hbm.1, s32[32]{0:T(128)} %prompt_hbm.1, s32[32]{0:T(128)} %rank_hbm.1, s32[32]{0:T(128)} %len_hbm.1, s32[64]{0:T(128)} %slot_hbm.1), custom_call_target="tpu_custom_call" | custom-call | flops 4026531840 | bytes 10485760 | tf_op jit(solution)/shard_map/pallas_call | solution.py:355
  53.9 0.7 %copy.11 = bf16[256,512]{1,0:T(8,128)(2,1)} copy(bf16[256,512]{1,0:T(8,128)(2,1)S(1)} %get-tuple-element.2) | data formatting | bytes 524288
  54.6 0.7 %copy.12 = bf16[2,128,256]{2,1,0:T(8,128)(2,1)} copy(bf16[2,128,256]{2,1,0:T(8,128)(2,1)S(1)} %get-tuple-element.3) | data formatting | bytes 262144
